TPU v7x, 128 devices: a whole 4x4x4 slice. The times are simulated.
128 devices in a mesh: row: 8 (over y_hi, x), col: 16 (over y_lo, z, core).
Axes of the slice: x: 4, y: 4 (y_hi: 2, y_lo: 2; y = y_hi * 2 + y_lo), z: 4, core: 2. Of those that a mesh axis runs over, the one named last changes fastest.
Arguments:
- series: bfloat16 [2048, 6144], P(('row', 'col')), may hold values from -6 to 6
- day_index: int32 [2048], P(('row', 'col')), may hold values from 0 to 364
- lags: int32 [8], replicated, may hold values from -28 to 28, as said below
Outputs:
- covariance: float32 [8, 6144, 6144], P(None, 'row', 'col')
Inputs may be any that keep to these rules, and one draw needn't show every extreme that they name: `lags`: both -28 and 28 are in the list.
All inputs are finite; a program needn't handle non-finite values.
Results may differ from a plain program's by a relative error of at most 0.0041.
Values may be sent and summed in bfloat16 or wider, within the bound.
A program may use at most 128 MiB of HBM per device.

v0:
```python
import math

import jax
import jax.numpy as jnp
from jax import lax
from jax.sharding import PartitionSpec as P

NLAG = 8
MAXLAG = 28
DAYS = 365


def shards(series, day_index, lags):
    n_row = lax.axis_size("row")
    n_col = lax.axis_size("col")
    steps_here, chans = series.shape
    total = steps_here * n_row * n_col
    rank = lax.axis_index("row") * n_col + lax.axis_index("col")
    day_grid = lax.broadcasted_iota(jnp.int32, (DAYS, steps_here), 0)
    onehot = (day_grid == day_index[None, :]).astype(jnp.float32)
    values = series.astype(jnp.float32)
    day_sums = jnp.dot(onehot, values, precision=lax.Precision.HIGHEST)
    day_counts = jnp.sum(onehot, axis=1)
    day_sums, day_counts = lax.psum((day_sums, day_counts), ("row", "col"))
    climate = day_sums / jnp.maximum(day_counts, 1.0)[:, None]
    season = jnp.dot(onehot.T, climate, precision=lax.Precision.HIGHEST)
    times = (rank * steps_here + jnp.arange(steps_here)).astype(jnp.float32)
    taper = 0.5 - 0.5 * jnp.cos(2.0 * math.pi * (times + 0.5) / total)
    moving = ((values - season) * taper[:, None]).astype(jnp.bfloat16)
    row_width = chans // n_row
    col_width = chans // n_col
    whole = lax.all_gather(moving, ("row", "col"), axis=0, tiled=True)
    row_part = lax.dynamic_slice_in_dim(whole, lax.axis_index("row") * row_width, row_width, 1)
    col_part = lax.dynamic_slice_in_dim(whole, lax.axis_index("col") * col_width, col_width, 1)
    padded = jnp.pad(col_part, ((MAXLAG, MAXLAG), (0, 0)))
    shifted_list = [
        lax.dynamic_slice_in_dim(padded, MAXLAG + lags[k], total, 0) for k in range(NLAG)
    ]
    contract = (((0,), (0,)), ((), ()))
    result = jnp.stack(
        [
            lax.dot_general(row_part, shifted, contract, preferred_element_type=jnp.float32)
            for shifted in shifted_list
        ]
    )
    return result / total


def solution(mesh):
    placed = (P(("row", "col"), None), P(("row", "col")), P())
    return jax.shard_map(
        shards, mesh=mesh, in_specs=placed, out_specs=P(None, "row", "col"), check_vma=False
    )
```

profile of v0, /device:TPU:1, one launch (start us, length us, event | category | flops | bytes accessed | tf_op | source)
XLA Modules:
  0.0 449.2 jit_solution(1324764659479045833)
XLA Ops:
  6.5 0.0 all-reduce.3.cloned.1.call-start
  6.5 6.0 %fusion.92 = f32[365,6144]{1,0:T(8,128)} fusion(bf16[16,6144]{1,0:T(8,128)(2,1)} %param.3, s32[16]{0:T(128)} %param.4), kind=kOutput, calls=%fused_computation.57 | convolution fusion | flops 71767760 | bytes 9166912 | tf_op jit(solution)/shard_map/dot_general | solution.py:22
  12.5 0.0 copy-start.3
  12.5 0.0 copy-start
  12.5 0.0 all-reduce.3.cloned.1.call-update
  12.6 0.0 all-gather.2.cloned.1.call-start
  12.6 0.6 copy-done.3
  13.2 0.1 convert_reduce_fusion
  13.3 69.1 %psum.15 = f32[365]{0:T(512)S(1)} all-reduce(f32[365]{0:T(512)S(1)} %convert_reduce_fusion), channel_id=1, replica_groups=mesh['row'=8,'col'=16] {'row','col'}, use_global_device_ids=true, to_apply=%region_2.0 | all-reduce | flops 365 | bytes 2920 | tf_op jit(solution)/shard_map/psum | solution.py:24
  82.5 0.0 copy-start.2
  82.5 96.8 %all-reduce.3.cloned.1.call-done = f32[365,6144]{1,0:T(8,128)} async-done(((f32[365,6144]{1,0:T(8,128)}), f32[365,6144]{1,0:T(8,128)}) %all-reduce.3.cloned.1.call-update) | async-done | bytes 8970256 | tf_op jit(solution)/shard_map/psum | solution.py:24
  179.3 0.0 copy-done
  179.3 7.6 %fusion.8 = bf16[16,6144]{1,0:T(8,128)(2,1)} fusion(f32[365,6144]{1,0:T(8,128)} %all-reduce.3.cloned.1.call-done, f32[365]{0:T(512)S(1)} %broadcast_maximum_fusion, bf16[16,6144]{1,0:T(8,128)(2,1)S(1)} %copy-done, f32[16]{0:T(128)S(1)} %multiply_subtract_fusion, s32[16]{0:T(128)S(1)} %copy-done.3), kind=kOutput, calls=%fused_computation.4 | convolution fusion | flops 433213120 | bytes 9365044 | tf_op jit(solution)/shard_map/dot_general | solution.py:26
  186.8 0.0 all-gather.2.cloned.1.call-update
  186.9 0.0 copy-done.2
  186.9 0.7 fusion.111
  197.2 215.4 %all-gather.2.cloned.1.call-done = bf16[2048,6144]{1,0:T(8,128)(2,1)} async-done(((bf16[16,6144]{1,0:T(8,128)(2,1)}), bf16[2048,6144]{1,0:T(8,128)(2,1)}) %all-gather.2.cloned.1.call-update) | async-done | bytes 25165840 | tf_op jit(solution)/shard_map/all_gather | solution.py:32
  412.6 0.0 copy-start.1
  412.6 1.7 constant_dynamic-slice_fusion
  414.3 4.0 fusion.31
  418.4 4.5 %fusion.37 = f32[8,768,384]{2,1,0:T(8,128)S(1)} fusion(f32[8,768,384]{2,1,0:T(8,128)S(1)} %fusion.31, s32[]{:T(128)S(6)} %select_n.33, bf16[2048,6144]{1,0:T(8,128)(2,1)} %all-gather.2.cloned.1.call-done, s32[]{:T(128)S(6)} %select_n.30, bf16[2048,384]{1,0:T(8,128)(2,1)S(1)} %constant_dynamic-slice_fusion), kind=kOutput, calls=%fused_computation.26 | convolution fusion | flops 1207959552 | bytes 5898248 | tf_op jit(solution)/shard_map/dot_general | solution.py:42
  422.9 3.7 fusion.43
  426.6 3.7 fusion.49
  430.3 0.0 copy-done.1
  430.3 1.9 fusion.55
  432.2 2.1 fusion.61
  434.3 1.8 fusion.67
  436.1 1.9 fusion.73
  437.9 4.5 broadcast_multiply_fusion
  (2 shorter events, 0.0 us)
Async XLA Ops:
  6.5 172.7 %all-reduce.3.cloned.1.call-start = ((), (), s32[]{:S(2)}) async-start(), calls=%async_computation | async-start | bytes 18087936 | tf_op jit(solution)/shard_map/psum | solution.py:24
  12.5 0.7 copy-start.3
  12.5 166.7 %copy-start = (bf16[16,6144]{1,0:T(8,128)(2,1)S(1)}, bf16[16,6144]{1,0:T(8,128)(2,1)}, u32[]{:S(2)}) copy-start(bf16[16,6144]{1,0:T(8,128)(2,1)} %param.3) | copy-start | bytes 589828
  12.6 400.0 %all-gather.2.cloned.1.call-start = ((), (), s32[]{:S(2)}) async-start(), calls=%async_computation.1 | async-start | bytes 25362432 | tf_op jit(solution)/shard_map/all_gather | solution.py:32
  82.5 104.4 %copy-start.2 = (s32[8]{0:T(128)S(1)}, s32[8]{0:T(128)}, u32[]{:S(2)}) copy-start(s32[8]{0:T(128)} %param.5) | copy-start | bytes 100
  412.6 17.7 %copy-start.1 = (bf16[2048,6144]{1,0:T(8,128)(2,1)S(1)}, bf16[2048,6144]{1,0:T(8,128)(2,1)}, u32[]{:S(2)}) copy-start(bf16[2048,6144]{1,0:T(8,128)(2,1)} %all-gather.2.cloned.1.call-done) | copy-start | bytes 75497472
Sparse Core Ops, SparseCore 0:
  12.7 166.5 all-reduce.2
  187.0 225.5 all-gather.1
where the time goes:
time: 450 us; the launch traced here: 449 us
  waiting for transfers between devices  312 us (69%)
  blocking collectives  69.1 us (15%)
  matrix products  37.1 us (8%)
  between operations  23.2 us (5%)
  other arithmetic  4.59 us (1%)
    all_gather x1, waiting for transfers between devices, shards(): whole = lax.all_gather(moving, ('row', 'col'), axis=0, tiled=True)  215 us
    psum x1, waiting for transfers between devices, shards(): day_sums, day_counts = lax.psum((day_sums, day_counts), ('row', 'col'))  96.8 us
    psum x1, blocking collectives, shards(): day_sums, day_counts = lax.psum((day_sums, day_counts), ('row', 'col'))  69.1 us
    dot_general x8, matrix products, shards(): lax.dot_general(row_part, shifted, contract, preferred_element_type=jnp.f...  23.6 us
  transfers between devices with their start and end apart: 2, of which 2 were waited for; matrix products, arithmetic and copies ran while one was open for 0% of the time, Pallas kernels for 0%

commit v1 on v0

v1 whole, which is shorter than its diff:
```python
import math

import jax
import jax.numpy as jnp
from jax import lax
from jax.experimental import pallas as pl
from jax.experimental.pallas import tpu as pltpu
from jax.sharding import PartitionSpec as P

NLAG = 8
DAYS = 384
TIME = 2048
NROW = 8
NCOL = 16
NDEV = NROW * NCOL
STEPS = 16
CHANS = 6144
ROWW = 768
COLW = 384
OWN = 48
PAD = 32
MESH = pl.DeviceIdType.MESH
F32 = jnp.float32
BF16 = jnp.bfloat16


class Ring:
    def __init__(self, ref, slot, device, p, q, send, recv):
        self.ref, self.slot, self.device = ref, slot, device
        self.p, self.q, self.send, self.recv = p, q, send, recv
        self.copies = {}

    def at(self, dq):
        return lax.rem(self.q + dq + 4, 4)

    def view(self, slot):
        return self.ref.at[pl.ds(pl.multiple_of(slot * OWN, 16), OWN)]

    def half(self, slot, h):
        lanes = pl.ds(h * (TIME // 2), TIME // 2)
        return self.ref.at[pl.ds(pl.multiple_of(slot * OWN, 16), OWN), lanes]

    def copy(self, n, ref, dev):
        copy = pltpu.make_async_remote_copy(
            src_ref=ref,
            dst_ref=ref,
            send_sem=self.send.at[n],
            recv_sem=self.recv.at[n],
            device_id=dev,
            device_id_type=MESH,
        )
        copy.start()
        self.copies[n] = copy

    def own(self):
        ref = self.view(self.slot(self.p, self.q))
        self.copy(1, ref, self.device(self.p, self.at(1)))
        self.copy(2, ref, self.device(self.p, self.at(-1)))
        self.copy(0, ref, self.device(1 - self.p, self.q))

    def other(self):
        self.copies[0].wait_recv()
        ref = self.view(self.slot(1 - self.p, self.q))
        self.copy(3, ref, self.device(self.p, self.at(1)))
        self.copy(4, ref, self.device(self.p, self.at(-1)))

    def forward(self, n):
        self.copies[n].wait_recv()
        pair = self.p if n < 3 else 1 - self.p
        if n % 2 == 1:
            ref = self.half(self.slot(pair, self.at(-1)), 0)
            self.copy(n + 4, ref, self.device(self.p, self.at(1)))
        else:
            ref = self.half(self.slot(pair, self.at(1)), 1)
            self.copy(n + 4, ref, self.device(self.p, self.at(-1)))


def dot(a, b):
    return jnp.dot(a, b, preferred_element_type=F32)


def split(x):
    high = x.astype(BF16)
    return high, (x - high.astype(F32)).astype(BF16)


def pick(held, start, to, lane):
    tile, off = divmod(start, 128)
    first = held[:, tile * 128 : (tile + 1) * 128].astype(F32)
    got = pltpu.roll(first, (to - off) % 128, 1)
    if off + OWN > 128:
        second = held[:, (tile + 1) * 128 : (tile + 2) * 128].astype(F32)
        got = jnp.where(lane < to + 128 - off, got, pltpu.roll(second, (to - off) % 128, 1))
    return got


def gather_kernel(
    series, days, lags, at, pad, lagv,
    held, held_days, held_lags, stage, land, xt, onehot, bt,
    sl, ss, rs, sra, rra, srb, rrb, ssib, rsib,
):
    r = lax.axis_index("row")
    c = lax.axis_index("col")
    rank = r * NCOL + c
    loads = [
        pltpu.make_async_copy(series, held, sl.at[0]),
        pltpu.make_async_copy(days, held_days, sl.at[1]),
        pltpu.make_async_copy(lags, held_lags, sl.at[2]),
    ]
    for load in loads:
        load.start()
    barrier = pltpu.get_barrier_semaphore()

    @pl.loop(1, NDEV)
    def _(j):
        to = lax.rem(rank + j, NDEV)
        pl.semaphore_signal(barrier, inc=1, device_id=(to // NCOL, lax.rem(to, NCOL)), device_id_type=MESH)

    for load in loads:
        load.wait()
    step = lax.broadcasted_iota(jnp.int32, (STEPS, 128), 0)
    lane = lax.broadcasted_iota(jnp.int32, (STEPS, 128), 1)
    day = jnp.zeros((STEPS, 128), jnp.int32)
    for i in range(STEPS):
        day = jnp.where(step == i, held_days[i], day)
    high = jnp.right_shift(day, 8)
    info = jnp.where(lane == 96, high, jnp.where(lane == 97, day - high * 256, jnp.where(lane == 98, 1, 0)))
    info = info.astype(F32)
    for d in range(NDEV):
        mine = pick(held, OWN * d, 0, lane)
        theirs = pick(held, COLW * (d % NCOL) + OWN * (d // NCOL), OWN, lane)
        row = jnp.where(lane < OWN, mine, jnp.where(lane < 2 * OWN, theirs, info))
        stage[d] = row.astype(BF16)
    for k in range(NLAG):
        lagv[k : k + 1, :] = jnp.full((1, 128), held_lags[k], jnp.int32).astype(F32)

    pl.semaphore_wait(barrier, NDEV - 1)

    @pl.loop(1, NDEV)
    def _(j):
        to = lax.rem(rank + j, NDEV)
        pltpu.make_async_remote_copy(
            src_ref=stage.at[to],
            dst_ref=land.at[rank],
            send_sem=ss,
            recv_sem=rs,
            device_id=(to // NCOL, lax.rem(to, NCOL)),
            device_id_type=MESH,
        ).start()

    land[rank] = stage[rank]
    when = lax.broadcasted_iota(jnp.int32, (NCOL, 128), 0) * 128 + lax.broadcasted_iota(jnp.int32, (NCOL, 128), 1)
    taper = 0.5 - 0.5 * jnp.cos(2.0 * math.pi * (when.astype(F32) + 0.5) / TIME)
    pad[:, :PAD, :] = jnp.zeros((3, PAD, 128), F32)
    pad[:, PAD + TIME :, :] = jnp.zeros((3, PAD, 128), F32)
    everyone = pltpu.make_async_remote_copy(
        src_ref=stage.at[0 : NDEV - 1],
        dst_ref=land.at[0 : NDEV - 1],
        send_sem=ss,
        recv_sem=rs,
        device_id=(r, c),
        device_id_type=MESH,
    )
    everyone.wait_recv()

    down = lax.broadcasted_iota(jnp.int32, (DAYS, 128), 0).astype(F32)
    for k in range(NCOL):
        here = land[8 * k : 8 * k + 8].reshape(128, 128).astype(F32).T
        lanes = slice(k * 128, (k + 1) * 128)
        xt[:, lanes] = here[: 2 * OWN]
        day_row = here[96:97] * 256.0 + here[97:98]
        onehot[:, lanes] = jnp.where(down == day_row, 1.0, 0.0).astype(BF16)
    sums = dot(onehot[...], land[...].reshape(TIME, 128))
    climate = sums * (1.0 / jnp.maximum(sums[:, 98:99], 1.0))
    high, low = split(climate.T[: 2 * OWN])
    both = jnp.concatenate([high, low], axis=0)
    for n in range(4):
        season = dot(both, onehot[:, n * 512 : (n + 1) * 512])
        season = season[: 2 * OWN] + season[2 * OWN :]
        for i in range(4):
            k = 4 * n + i
            lanes = slice(k * 128, (k + 1) * 128)
            anomaly = (xt[:, lanes] - season[:, i * 128 : (i + 1) * 128]) * taper[k : k + 1]
            anomaly = anomaly.astype(BF16)
            at[pl.ds(pl.multiple_of(c * OWN, 16), OWN), lanes] = anomaly[:OWN]
            bt[pl.ds(pl.multiple_of(r * OWN, 16), OWN), lanes] = anomaly[OWN:]

    core = lax.rem(c, 2)
    ring_a = Ring(
        at,
        lambda p, q: p * 8 + q * 2 + core,
        lambda p, q: (r, p * 8 + q * 2 + core),
        c // 8,
        lax.rem(c // 2, 4),
        sra,
        rra,
    )
    ring_b = Ring(
        bt,
        lambda p, q: p * 4 + q,
        lambda p, q: (p * 4 + q, c),
        r // 4,
        lax.rem(r, 4),
        srb,
        rrb,
    )
    siblings = []

    def sibling(p, q):
        n = len(siblings)
        ref = ring_a.view(ring_a.slot(p, q))
        copy = pltpu.make_async_remote_copy(
            src_ref=ref,
            dst_ref=ref,
            send_sem=ssib.at[n],
            recv_sem=rsib.at[n],
            device_id=(r, c + 1 - 2 * core),
            device_id_type=MESH,
        )
        copy.start()
        siblings.append(copy)

    ring_a.own()
    ring_b.own()
    pa, qa = ring_a.p, ring_a.q
    sibling(pa, qa)
    ring_a.other()
    ring_b.other()
    for n in (1, 2):
        ring_a.forward(n)
        ring_b.forward(n)
    sibling(1 - pa, qa)
    sibling(pa, ring_a.at(-1))
    sibling(pa, ring_a.at(1))
    for n in (3, 4):
        ring_a.forward(n)
        ring_b.forward(n)
    sibling(1 - pa, ring_a.at(-1))
    sibling(1 - pa, ring_a.at(1))
    for n in (5, 6):
        ring_a.copies[n].wait_recv()
    sibling(pa, ring_a.at(2))
    for n in (7, 8):
        ring_a.copies[n].wait_recv()
    sibling(1 - pa, ring_a.at(2))
    for n in (5, 6, 7, 8):
        ring_b.copies[n].wait_recv()
    for w in range(3):
        for k in range(NCOL):
            tile = bt[w * 128 : (w + 1) * 128, k * 128 : (k + 1) * 128].astype(F32)
            pad[w, PAD + k * 128 : PAD + (k + 1) * 128, :] = tile.T
    for copy in siblings:
        copy.wait()
    everyone.wait_send()
    for copy in list(ring_a.copies.values()) + list(ring_b.copies.values()):
        copy.wait_send()


def gather(series, day_index, lags):
    dma = pltpu.SemaphoreType.DMA
    hbm = pl.BlockSpec(memory_space=pltpu.HBM)
    vmem = pl.BlockSpec(memory_space=pltpu.VMEM)
    return pl.pallas_call(
        gather_kernel,
        out_shape=(
            jax.ShapeDtypeStruct((ROWW, TIME), BF16),
            jax.ShapeDtypeStruct((3, TIME + 2 * PAD, 128), F32),
            jax.ShapeDtypeStruct((NLAG, 128), F32),
        ),
        in_specs=[hbm, hbm, hbm],
        out_specs=(vmem, vmem, vmem),
        scratch_shapes=[
            pltpu.VMEM((STEPS, CHANS), BF16),
            pltpu.SMEM((STEPS,), jnp.int32),
            pltpu.SMEM((NLAG,), jnp.int32),
            pltpu.VMEM((NDEV, STEPS, 128), BF16),
            pltpu.VMEM((NDEV, STEPS, 128), BF16),
            pltpu.VMEM((2 * OWN, TIME), F32),
            pltpu.VMEM((DAYS, TIME), BF16),
            pltpu.VMEM((COLW, TIME), BF16),
            dma((3,)),
            dma(()),
            dma(()),
            dma((9,)),
            dma((9,)),
            dma((9,)),
            dma((9,)),
            dma((8,)),
            dma((8,)),
        ],
        compiler_params=pltpu.CompilerParams(
            collective_id=0, has_side_effects=True, vmem_limit_bytes=24 * 2**20
        ),
        name="gather_anomaly",
    )(series, day_index, lags)


def cov_kernel(at, pad, lagv, out, even, odd):
    g = pl.program_id(0)
    m = pl.program_id(1)

    def fill(pair, first, count, held):
        for i in range(2):
            lag = jnp.max(lagv[pl.ds(2 * pair + i, 1), :]).astype(jnp.int32)
            for w in range(3):
                lanes = slice(i * COLW + w * 128, i * COLW + (w + 1) * 128)
                piece = pad[w, pl.ds(first + PAD + lag, count), :]
                held[pl.ds(first, count), lanes] = piece.astype(BF16)

    @pl.when((g == 0) & (m == 0))
    def _():
        fill(0, 0, TIME, even)

    def body(now, later):
        fill(lax.rem(g + 1, NLAG // 2), pl.multiple_of(m * (TIME // 2), TIME // 2), TIME // 2, later)
        prod = dot(at[pl.ds(pl.multiple_of(m * 384, 384), 384), :], now[...]) * (1.0 / TIME)
        out[0] = prod[:, :COLW]
        out[1] = prod[:, COLW:]

    @pl.when(lax.rem(g, 2) == 0)
    def _():
        body(even, odd)

    @pl.when(lax.rem(g, 2) == 1)
    def _():
        body(odd, even)


def covariance(at, pad, lagv):
    once = pl.Buffered(1)
    return pl.pallas_call(
        cov_kernel,
        grid=(NLAG // 2, 2),
        out_shape=jax.ShapeDtypeStruct((NLAG, ROWW, COLW), F32),
        in_specs=[
            pl.BlockSpec((ROWW, TIME), lambda g, m: (0, 0), pipeline_mode=once),
            pl.BlockSpec((3, TIME + 2 * PAD, 128), lambda g, m: (0, 0, 0), pipeline_mode=once),
            pl.BlockSpec((NLAG, 128), lambda g, m: (0, 0), pipeline_mode=once),
        ],
        out_specs=pl.BlockSpec((2, ROWW // 2, COLW), lambda g, m: (g, m, 0)),
        scratch_shapes=[
            pltpu.VMEM((TIME, 2 * COLW), BF16),
            pltpu.VMEM((TIME, 2 * COLW), BF16),
        ],
        compiler_params=pltpu.CompilerParams(
            dimension_semantics=("arbitrary", "arbitrary"), vmem_limit_bytes=36 * 2**20
        ),
        name="lagged_covariance",
    )(at, pad, lagv)


def shards(series, day_index, lags):
    return covariance(*gather(series, day_index, lags))


def solution(mesh):
    placed = (P(("row", "col"), None), P(("row", "col")), P())
    return jax.shard_map(
        shards, mesh=mesh, in_specs=placed, out_specs=P(None, "row", "col"), check_vma=False
    )
```

time: 450 us -> 63.7 us (0.14)
  waiting for transfers between devices: 312 us -> 0 us
  blocking collectives: 69.1 us -> 0 us
  Pallas kernels: 0 us -> 61.3 us
  matrix products: 37.1 us -> 0 us
  between operations: 23.2 us -> 0.01 us
  other arithmetic: 4.59 us -> 0 us
    all_gather x1 -> x0, waiting for transfers between devices: 215 us -> none  [shards(): whole = lax.all_gather(moving, ('row', 'col'), axis=0, tiled=True)]
    psum x1 -> x0, waiting for transfers between devices: 96.8 us -> none  [shards(): day_sums, day_counts = lax.psum((day_sums, day_counts), ('row', 'col'))]
    psum x1 -> x0, blocking collectives: 69.1 us -> none  [shards(): day_sums, day_counts = lax.psum((day_sums, day_counts), ('row', 'col'))]
    pallas_call x0 -> x2, Pallas kernels: none -> 61.3 us  [the longest x1 47 us: gather(): pl.pallas_call(gather_kernel, out_shape=(jax.ShapeDtypeStruct((ROWW, TIME...]
    dot_general x10 -> x0, matrix products: 37.1 us -> none  [the longest x8 23.6 us: shards(): lax.dot_general(row_part, shifted, contract, preferred_element_type=jnp.f...]
  transfers between devices with their start and end apart: 2 -> 0, of which waited for: 2 -> 0; matrix products, arithmetic and copies ran while one was open for 0% -> 0% of each run, Pallas kernels for 0% -> 0%
where the time goes in v1:
time: 63.7 us; the launch traced here: 63.5 us
  Pallas kernels  61.3 us (96%)
  local copies, waits for them, and re-layouts  2.24 us (4%)
    pallas_call x1, Pallas kernels, gather(): pl.pallas_call(gather_kernel, out_shape=(jax.ShapeDtypeStruct((ROWW, TIME...  47 us
    pallas_call x1, Pallas kernels, covariance(): pl.pallas_call(cov_kernel, grid=(NLAG // 2, 2), out_shape=jax.ShapeDtypeS...  14.3 us
    unnamed x6, local copies, waits for them, and re-layouts  2.24 us

profile of v1, /device:TPU:1, one launch (start us, length us, event | category | flops | bytes accessed | tf_op | source)
XLA Modules:
  0.0 63.5 jit_solution(976419647056948089)
XLA Ops:
  0.0 0.0 copy-start
  0.0 0.9 %copy-done = bf16[16,6144]{1,0:T(8,128)(2,1)S(1)} copy-done((bf16[16,6144]{1,0:T(8,128)(2,1)S(1)}, bf16[16,6144]{1,0:T(8,128)(2,1)}, u32[]{:S(2)}) %copy-start) | copy-done | bytes 196632
  0.9 0.0 copy-start.1
  0.9 0.7 %copy-done.1 = s32[16]{0:T(128)S(1)} copy-done((s32[16]{0:T(128)S(1)}, s32[16]{0:T(128)}, u32[]{:S(2)}) %copy-start.1) | copy-done | bytes 88
  1.6 0.0 copy-start.2
  1.6 0.7 %copy-done.2 = s32[8]{0:T(128)S(1)} copy-done((s32[8]{0:T(128)S(1)}, s32[8]{0:T(128)}, u32[]{:S(2)}) %copy-start.2) | copy-done | bytes 56
  2.2 47.0 %gather_anomaly.1 = (bf16[768,2048]{1,0:T(8,128)(2,1)S(1)}, f32[3,2112,128]{2,1,0:T(8,128)S(1)}, f32[8,128]{1,0:T(8,128)S(1)}) custom-call(bf16[16,6144]{1,0:T(8,128)(2,1)S(1)} %copy-done, s32[16]{0:T(128)S(1)} %copy-done.1, s32[8]{0:T(128)S(1)} %copy-done.2), custom_call_target="tpu_custom_call" | custom-call | tf_op jit(solution)/shard_map/gather_anomaly/pallas_call | solution.py:263
  49.2 14.3 %lagged_covariance.1 = f32[8,768,384]{2,1,0:T(8,128)} custom-call(bf16[768,2048]{1,0:T(8,128)(2,1)S(1)} %get-tuple-element.8.at, f32[3,2112,128]{2,1,0:T(8,128)S(1)} %get-tuple-element.9.pad, f32[8,128]{1,0:T(8,128)S(1)} %get-tuple-element.10.lagv), custom_call_target="tpu_custom_call" | custom-call | tf_op jit(solution)/shard_map/lagged_covariance/pallas_call | solution.py:331
Async XLA Ops:
  0.0 0.9 %copy-start = (bf16[16,6144]{1,0:T(8,128)(2,1)S(1)}, bf16[16,6144]{1,0:T(8,128)(2,1)}, u32[]{:S(2)}) copy-start(bf16[16,6144]{1,0:T(8,128)(2,1)} %series.1) | copy-start | bytes 589828
  0.9 0.7 %copy-start.1 = (s32[16]{0:T(128)S(1)}, s32[16]{0:T(128)}, u32[]{:S(2)}) copy-start(s32[16]{0:T(128)} %days.1) | copy-start | bytes 196
  1.6 0.7 %copy-start.2 = (s32[8]{0:T(128)S(1)}, s32[8]{0:T(128)}, u32[]{:S(2)}) copy-start(s32[8]{0:T(128)} %lags.1) | copy-start | bytes 100

commit v2 on v1

--- a/solution.py
+++ b/solution.py
@@ -19,6 +19,10 @@
 COLW = 384
 OWN = 48
 PAD = 32
+CHUNKS = ((0, 640), (640, 512), (1152, 512), (1664, 384))
+HALVES = (384, 256, 256, 128)
+WINDOW = 512
+PAIRS = NLAG // 2
 MESH = pl.DeviceIdType.MESH
 F32 = jnp.float32
 BF16 = jnp.bfloat16
@@ -33,46 +37,53 @@
     def at(self, dq):
         return lax.rem(self.q + dq + 4, 4)
 
-    def view(self, slot):
-        return self.ref.at[pl.ds(pl.multiple_of(slot * OWN, 16), OWN)]
-
-    def half(self, slot, h):
-        lanes = pl.ds(h * (TIME // 2), TIME // 2)
-        return self.ref.at[pl.ds(pl.multiple_of(slot * OWN, 16), OWN), lanes]
-
-    def copy(self, n, ref, dev):
+    def view(self, slot, j, half=None):
+        start, size = CHUNKS[j]
+        if half == 0:
+            size = HALVES[j]
+        elif half == 1:
+            start, size = start + HALVES[j], size - HALVES[j]
+        return self.ref.at[pl.ds(pl.multiple_of(slot * OWN, 16), OWN), start : start + size]
+
+    def copy(self, j, n, ref, dev):
         copy = pltpu.make_async_remote_copy(
             src_ref=ref,
             dst_ref=ref,
-            send_sem=self.send.at[n],
-            recv_sem=self.recv.at[n],
+            send_sem=self.send.at[j, n],
+            recv_sem=self.recv.at[j, n],
             device_id=dev,
             device_id_type=MESH,
         )
         copy.start()
-        self.copies[n] = copy
-
-    def own(self):
-        ref = self.view(self.slot(self.p, self.q))
-        self.copy(1, ref, self.device(self.p, self.at(1)))
-        self.copy(2, ref, self.device(self.p, self.at(-1)))
-        self.copy(0, ref, self.device(1 - self.p, self.q))
-
-    def other(self):
-        self.copies[0].wait_recv()
-        ref = self.view(self.slot(1 - self.p, self.q))
-        self.copy(3, ref, self.device(self.p, self.at(1)))
-        self.copy(4, ref, self.device(self.p, self.at(-1)))
-
-    def forward(self, n):
-        self.copies[n].wait_recv()
+        self.copies[j, n] = copy
+
+    def across(self, j):
+        self.copy(j, 0, self.view(self.slot(self.p, self.q), j), self.device(1 - self.p, self.q))
+
+    def own(self, j):
+        ref = self.view(self.slot(self.p, self.q), j)
+        self.copy(j, 1, ref, self.device(self.p, self.at(1)))
+        self.copy(j, 2, ref, self.device(self.p, self.at(-1)))
+
+    def other(self, j):
+        self.copies[j, 0].wait_recv()
+        ref = self.view(self.slot(1 - self.p, self.q), j)
+        self.copy(j, 3, ref, self.device(self.p, self.at(1)))
+        self.copy(j, 4, ref, self.device(self.p, self.at(-1)))
+
+    def forward(self, j, n):
+        self.copies[j, n].wait_recv()
         pair = self.p if n < 3 else 1 - self.p
         if n % 2 == 1:
-            ref = self.half(self.slot(pair, self.at(-1)), 0)
-            self.copy(n + 4, ref, self.device(self.p, self.at(1)))
+            self.copy(j, n + 4, self.view(self.slot(pair, self.at(-1)), j, 0), self.device(self.p, self.at(1)))
         else:
-            ref = self.half(self.slot(pair, self.at(1)), 1)
-            self.copy(n + 4, ref, self.device(self.p, self.at(-1)))
+            self.copy(j, n + 4, self.view(self.slot(pair, self.at(1)), j, 1), self.device(self.p, self.at(-1)))
+
+
+def fill(pad, lag, i, first, count, held):
+    for w in range(3):
+        piece = pad[w, pl.ds(first + PAD + lag, count), :]
+        held[:, i * COLW + w * 128 : i * COLW + (w + 1) * 128] = piece.astype(BF16)
 
 
 def dot(a, b):
@@ -95,8 +106,8 @@
 
 
 def gather_kernel(
-    series, days, lags, at, pad, lagv,
-    held, held_days, held_lags, stage, land, xt, onehot, bt,
+    series, days, lags, at, pad, lagv, part,
+    held, held_days, held_lags, stage, land, xt, onehot, bt, even, odd,
     sl, ss, rs, sra, rra, srb, rrb, ssib, rsib,
 ):
     r = lax.axis_index("row")
@@ -204,55 +215,118 @@
         srb,
         rrb,
     )
-    siblings = []
-
-    def sibling(p, q):
-        n = len(siblings)
-        ref = ring_a.view(ring_a.slot(p, q))
+    siblings = {}
+    pa, qa = ring_a.p, ring_a.q
+
+    def sibling(j, p, q):
+        n = sum(key[0] == j for key in siblings)
+        ref = ring_a.view(ring_a.slot(p, q), j)
         copy = pltpu.make_async_remote_copy(
             src_ref=ref,
             dst_ref=ref,
-            send_sem=ssib.at[n],
-            recv_sem=rsib.at[n],
+            send_sem=ssib.at[j, n],
+            recv_sem=rsib.at[j, n],
             device_id=(r, c + 1 - 2 * core),
             device_id_type=MESH,
         )
         copy.start()
-        siblings.append(copy)
-
-    ring_a.own()
-    ring_b.own()
-    pa, qa = ring_a.p, ring_a.q
-    sibling(pa, qa)
-    ring_a.other()
-    ring_b.other()
-    for n in (1, 2):
-        ring_a.forward(n)
-        ring_b.forward(n)
-    sibling(1 - pa, qa)
-    sibling(pa, ring_a.at(-1))
-    sibling(pa, ring_a.at(1))
-    for n in (3, 4):
-        ring_a.forward(n)
-        ring_b.forward(n)
-    sibling(1 - pa, ring_a.at(-1))
-    sibling(1 - pa, ring_a.at(1))
-    for n in (5, 6):
-        ring_a.copies[n].wait_recv()
-    sibling(pa, ring_a.at(2))
-    for n in (7, 8):
-        ring_a.copies[n].wait_recv()
-    sibling(1 - pa, ring_a.at(2))
-    for n in (5, 6, 7, 8):
-        ring_b.copies[n].wait_recv()
-    for w in range(3):
-        for k in range(NCOL):
-            tile = bt[w * 128 : (w + 1) * 128, k * 128 : (k + 1) * 128].astype(F32)
-            pad[w, PAD + k * 128 : PAD + (k + 1) * 128, :] = tile.T
-    for copy in siblings:
-        copy.wait()
+        siblings[j, n] = copy
+
+    def own(j):
+        ring_a.own(j)
+        ring_b.own(j)
+        sibling(j, pa, qa)
+
+    def other(j):
+        ring_a.other(j)
+        ring_b.other(j)
+        sibling(j, 1 - pa, qa)
+
+    def near(j):
+        for n in (1, 2):
+            ring_a.forward(j, n)
+            ring_b.forward(j, n)
+        sibling(j, pa, ring_a.at(-1))
+        sibling(j, pa, ring_a.at(1))
+
+    def far(j):
+        for n in (3, 4):
+            ring_a.forward(j, n)
+            ring_b.forward(j, n)
+        sibling(j, 1 - pa, ring_a.at(-1))
+        sibling(j, 1 - pa, ring_a.at(1))
+
+    def last(j):
+        for n, p in ((5, pa), (7, 1 - pa)):
+            ring_a.copies[j, n].wait_recv()
+            ring_a.copies[j, n + 1].wait_recv()
+            sibling(j, p, ring_a.at(2))
+        for n in (5, 6, 7, 8):
+            ring_b.copies[j, n].wait_recv()
+
+    def turn(j):
+        start, size = CHUNKS[j]
+        for w in range(3):
+            for k in range(start, start + size, 128):
+                tile = bt[w * 128 : (w + 1) * 128, k : k + 128].astype(F32)
+                pad[w, PAD + k : PAD + k + 128, :] = tile.T
+
+    def close(j):
+        for n in range(8):
+            siblings[j, n].wait_recv()
+
+    def products(j, between):
+        first = j * WINDOW
+        for i in range(2):
+            fill(pad, held_lags[i], i, first, WINDOW, even)
+        for n in range(2 * PAIRS):
+            pair, m = n // 2, n % 2
+            now, later = (even, odd) if pair % 2 == 0 else (odd, even)
+            if pair + 1 < PAIRS:
+                fill(pad, held_lags[2 * pair + 2 + m], m, first, WINDOW, later)
+            prod = dot(at[m * 384 : (m + 1) * 384, first : first + WINDOW], now[...])
+            for i in range(2):
+                where = (2 * pair + i, slice(m * 384, (m + 1) * 384))
+                here = prod[:, i * COLW : (i + 1) * COLW]
+                part[where] = here if j == 0 else part[where] + here
+            for act in between.get(n, ()):
+                act()
+
+    for j in range(4):
+        ring_a.across(j)
+        ring_b.across(j)
+    own(0)
+    own(1)
+    near(0)
+    other(0)
+    own(2)
+    near(1)
+    far(0)
+    own(3)
+    other(1)
+    last(0)
+    turn(0)
+    close(0)
+    products(
+        0,
+        {
+            0: [lambda: near(2)],
+            2: [lambda: far(1)],
+            3: [lambda: other(2)],
+            5: [lambda: near(3)],
+            6: [lambda: last(1)],
+        },
+    )
+    turn(1)
+    close(1)
+    products(1, {1: [lambda: far(2)], 3: [lambda: other(3)], 5: [lambda: last(2)]})
+    turn(2)
+    close(2)
+    products(2, {2: [lambda: far(3)], 6: [lambda: last(3)]})
+    turn(3)
+    close(3)
     everyone.wait_send()
-    for copy in list(ring_a.copies.values()) + list(ring_b.copies.values()):
+    for copy in list(siblings.values()) + list(ring_a.copies.values()) + list(ring_b.copies.values()):
         copy.wait_send()
 
 
@@ -266,9 +340,10 @@
             jax.ShapeDtypeStruct((ROWW, TIME), BF16),
             jax.ShapeDtypeStruct((3, TIME + 2 * PAD, 128), F32),
             jax.ShapeDtypeStruct((NLAG, 128), F32),
+            jax.ShapeDtypeStruct((NLAG, ROWW, COLW), F32),
         ),
         in_specs=[hbm, hbm, hbm],
-        out_specs=(vmem, vmem, vmem),
+        out_specs=(vmem, vmem, vmem, vmem),
         scratch_shapes=[
             pltpu.VMEM((STEPS, CHANS), BF16),
             pltpu.SMEM((STEPS,), jnp.int32),
@@ -278,44 +353,49 @@
             pltpu.VMEM((2 * OWN, TIME), F32),
             pltpu.VMEM((DAYS, TIME), BF16),
             pltpu.VMEM((COLW, TIME), BF16),
+            pltpu.VMEM((WINDOW, 2 * COLW), BF16),
+            pltpu.VMEM((WINDOW, 2 * COLW), BF16),
             dma((3,)),
             dma(()),
             dma(()),
-            dma((9,)),
-            dma((9,)),
-            dma((9,)),
-            dma((9,)),
-            dma((8,)),
-            dma((8,)),
+            dma((4, 9)),
+            dma((4, 9)),
+            dma((4, 9)),
+            dma((4, 9)),
+            dma((4, 8)),
+            dma((4, 8)),
         ],
         compiler_params=pltpu.CompilerParams(
             collective_id=0, has_side_effects=True, vmem_limit_bytes=24 * 2**20
         ),
         name="gather_anomaly",
-    )(series, day_index, lags)
-
-
-def cov_kernel(at, pad, lagv, out, even, odd):
+    )(*(pltpu.with_memory_space_constraint(x, pltpu.HBM) for x in (series, day_index, lags)))
+
+
+def cov_kernel(at, pad, lagv, part, out, even, odd):
+    first = TIME - WINDOW
     g = pl.program_id(0)
     m = pl.program_id(1)
 
-    def fill(pair, first, count, held):
-        for i in range(2):
-            lag = jnp.max(lagv[pl.ds(2 * pair + i, 1), :]).astype(jnp.int32)
-            for w in range(3):
-                lanes = slice(i * COLW + w * 128, i * COLW + (w + 1) * 128)
-                piece = pad[w, pl.ds(first + PAD + lag, count), :]
-                held[pl.ds(first, count), lanes] = piece.astype(BF16)
+    def shift(pair, i, held):
+        lag = jnp.max(lagv[pl.ds(2 * pair + i, 1), :]).astype(jnp.int32)
+        fill(pad, lag, i, first, WINDOW, held)
 
     @pl.when((g == 0) & (m == 0))
     def _():
-        fill(0, 0, TIME, even)
+        shift(0, 0, even)
+        shift(0, 1, even)
 
     def body(now, later):
-        fill(lax.rem(g + 1, NLAG // 2), pl.multiple_of(m * (TIME // 2), TIME // 2), TIME // 2, later)
-        prod = dot(at[pl.ds(pl.multiple_of(m * 384, 384), 384), :], now[...]) * (1.0 / TIME)
-        out[0] = prod[:, :COLW]
-        out[1] = prod[:, COLW:]
+        for i in range(2):
+
+            @pl.when(m == i)
+            def _():
+                shift(lax.rem(g + 1, PAIRS), i, later)
+                rows = slice(i * 384, (i + 1) * 384)
+                prod = dot(at[rows, first:], now[...])
+                out[0] = (part[2 * g, rows] + prod[:, :COLW]) * (1.0 / TIME)
+                out[1] = (part[2 * g + 1, rows] + prod[:, COLW:]) * (1.0 / TIME)
 
     @pl.when(lax.rem(g, 2) == 0)
     def _():
@@ -326,27 +406,23 @@
         body(odd, even)
 
 
-def covariance(at, pad, lagv):
-    once = pl.Buffered(1)
+def covariance(at, pad, lagv, part):
+    vmem = pl.BlockSpec(memory_space=pltpu.VMEM)
     return pl.pallas_call(
         cov_kernel,
-        grid=(NLAG // 2, 2),
+        grid=(PAIRS, 2),
         out_shape=jax.ShapeDtypeStruct((NLAG, ROWW, COLW), F32),
-        in_specs=[
-            pl.BlockSpec((ROWW, TIME), lambda g, m: (0, 0), pipeline_mode=once),
-            pl.BlockSpec((3, TIME + 2 * PAD, 128), lambda g, m: (0, 0, 0), pipeline_mode=once),
-            pl.BlockSpec((NLAG, 128), lambda g, m: (0, 0), pipeline_mode=once),
-        ],
+        in_specs=[vmem] * 4,
         out_specs=pl.BlockSpec((2, ROWW // 2, COLW), lambda g, m: (g, m, 0)),
         scratch_shapes=[
-            pltpu.VMEM((TIME, 2 * COLW), BF16),
-            pltpu.VMEM((TIME, 2 * COLW), BF16),
+            pltpu.VMEM((WINDOW, 2 * COLW), BF16),
+            pltpu.VMEM((WINDOW, 2 * COLW), BF16),
         ],
         compiler_params=pltpu.CompilerParams(
-            dimension_semantics=("arbitrary", "arbitrary"), vmem_limit_bytes=36 * 2**20
+            dimension_semantics=("arbitrary", "arbitrary"), vmem_limit_bytes=20 * 2**20
         ),
         name="lagged_covariance",
-    )(at, pad, lagv)
+    )(at, pad, lagv, part)
 
 
 def shards(series, day_index, lags):

time: 63.7 us -> 62.8 us (0.986)
  local copies, waits for them, and re-layouts: 2.24 us -> 0 us
  Pallas kernels: 61.3 us -> 62.7 us
    pallas_call x1, Pallas kernels: 47 us -> 55.7 us  [gather(): pl.pallas_call(gather_kernel, out_shape=(jax.ShapeDtypeStruct((ROWW, TIME...]
    pallas_call x1, Pallas kernels: 14.3 us -> 6.98 us  [covariance(): pl.pallas_call(cov_kernel, grid=(PAIRS, 2), out_shape=jax.ShapeDtypeStruc...]
    unnamed x6 -> x0, local copies, waits for them, and re-layouts: 2.24 us -> none
where the time goes in v2:
time: 62.8 us; the launch traced here: 62.7 us
  Pallas kernels  62.7 us (100%)
    pallas_call x1, Pallas kernels, gather(): pl.pallas_call(gather_kernel, out_shape=(jax.ShapeDtypeStruct((ROWW, TIME...  55.7 us
    pallas_call x1, Pallas kernels, covariance(): pl.pallas_call(cov_kernel, grid=(PAIRS, 2), out_shape=jax.ShapeDtypeStruc...  6.98 us

profile of v2, /device:TPU:1, one launch (start us, length us, event | category | flops | bytes accessed | tf_op | source)
XLA Modules:
  0.0 62.7 jit_solution(16013209436761278130)
XLA Ops:
  0.0 55.7 %gather_anomaly.1 = (bf16[768,2048]{1,0:T(8,128)(2,1)S(1)}, f32[3,2112,128]{2,1,0:T(8,128)S(1)}, f32[8,128]{1,0:T(8,128)S(1)}, f32[8,768,384]{2,1,0:T(8,128)S(1)}) custom-call(bf16[16,6144]{1,0:T(8,128)(2,1)} %series.1, s32[16]{0:T(128)} %days.1, s32[8]{0:T(128)} %lags.1), custom_call_target="tpu_custom_call" | custom-call | tf_op jit(solution)/shard_map/gather_anomaly/pallas_call | solution.py:337
  55.7 7.0 %lagged_covariance.1 = f32[8,768,384]{2,1,0:T(8,128)} custom-call(bf16[768,2048]{1,0:T(8,128)(2,1)S(1)} %get-tuple-element.9.at, f32[3,2112,128]{2,1,0:T(8,128)S(1)} %get-tuple-element.10.pad, f32[8,128]{1,0:T(8,128)S(1)} %get-tuple-element.11.lagv, f32[8,768,384]{2,1,0:T(8,128)S(1)} %get-tuple-element.12.part), custom_call_target="tpu_custom_call" | custom-call | tf_op jit(solution)/shard_map/lagged_covariance/pallas_call | solution.py:411

commit v3 on v2

--- a/solution.py
+++ b/solution.py
@@ -13,16 +13,19 @@
 NROW = 8
 NCOL = 16
 NDEV = NROW * NCOL
+NPAIR = NCOL // 2
+NCHIP = NDEV // 2
 STEPS = 16
 CHANS = 6144
 ROWW = 768
 COLW = 384
 OWN = 48
 PAD = 32
-CHUNKS = ((0, 640), (640, 512), (1152, 512), (1664, 384))
-HALVES = (384, 256, 256, 128)
-WINDOW = 512
+CHUNKS = ((0, 1152), (1152, 896))
+HALVES = (640, 384)
+WINDOW = 1024
 PAIRS = NLAG // 2
+SLOTS = 3
 MESH = pl.DeviceIdType.MESH
 F32 = jnp.float32
 BF16 = jnp.bfloat16
@@ -107,12 +110,17 @@
 
 def gather_kernel(
     series, days, lags, at, pad, lagv, part,
-    held, held_days, held_lags, stage, land, xt, onehot, bt, even, odd,
-    sl, ss, rs, sra, rra, srb, rrb, ssib, rsib,
+    held, held_days, held_lags, stage, mid, land, xt, onehot, bt, even, odd,
+    sl, ss, rs, sx, rx, sra, rra, srb, rrb, ssib, rsib,
 ):
     r = lax.axis_index("row")
     c = lax.axis_index("col")
-    rank = r * NCOL + c
+    core = lax.rem(c, 2)
+    chip = r * NPAIR + c // 2
+    to_r = [jnp.where(r + j >= NROW, r + j - NROW, r + j) for j in range(NROW)]
+    to_c = [jnp.where(c + 2 * j >= NCOL, c + 2 * j - NCOL, c + 2 * j) for j in range(NPAIR)]
+    to_p = [jnp.where(c // 2 + j >= NPAIR, c // 2 + j - NPAIR, c // 2 + j) for j in range(NPAIR)]
+    across = (r, c + 1 - 2 * core)
     loads = [
         pltpu.make_async_copy(series, held, sl.at[0]),
         pltpu.make_async_copy(days, held_days, sl.at[1]),
@@ -122,10 +130,11 @@
         load.start()
     barrier = pltpu.get_barrier_semaphore()
 
-    @pl.loop(1, NDEV)
-    def _(j):
-        to = lax.rem(rank + j, NDEV)
-        pl.semaphore_signal(barrier, inc=1, device_id=(to // NCOL, lax.rem(to, NCOL)), device_id_type=MESH)
+    for jr in range(NROW):
+        for jc in range(NPAIR):
+            if jr or jc:
+                pl.semaphore_signal(barrier, inc=1, device_id=(to_r[jr], to_c[jc]), device_id_type=MESH)
+    pl.semaphore_signal(barrier, inc=1, device_id=across, device_id_type=MESH)
 
     for load in loads:
         load.wait()
@@ -141,42 +150,51 @@
         mine = pick(held, OWN * d, 0, lane)
         theirs = pick(held, COLW * (d % NCOL) + OWN * (d // NCOL), OWN, lane)
         row = jnp.where(lane < OWN, mine, jnp.where(lane < 2 * OWN, theirs, info))
-        stage[d] = row.astype(BF16)
+        stage[d // 2, d % 2] = row.astype(BF16)
     for k in range(NLAG):
         lagv[k : k + 1, :] = jnp.full((1, 128), held_lags[k], jnp.int32).astype(F32)
 
-    pl.semaphore_wait(barrier, NDEV - 1)
-
-    @pl.loop(1, NDEV)
-    def _(j):
-        to = lax.rem(rank + j, NDEV)
-        pltpu.make_async_remote_copy(
-            src_ref=stage.at[to],
-            dst_ref=land.at[rank],
-            send_sem=ss,
-            recv_sem=rs,
-            device_id=(to // NCOL, lax.rem(to, NCOL)),
-            device_id_type=MESH,
-        ).start()
-
-    land[rank] = stage[rank]
+    pl.semaphore_wait(barrier, NCHIP)
+    for jr in range(NROW):
+        for jc in range(NPAIR):
+            if jr or jc:
+                pltpu.make_async_remote_copy(
+                    src_ref=stage.at[to_r[jr] * NPAIR + to_p[jc]],
+                    dst_ref=mid.at[chip],
+                    send_sem=ss,
+                    recv_sem=rs,
+                    device_id=(to_r[jr], to_c[jc]),
+                    device_id_type=MESH,
+                ).start()
+    mid[chip] = stage[chip]
     when = lax.broadcasted_iota(jnp.int32, (NCOL, 128), 0) * 128 + lax.broadcasted_iota(jnp.int32, (NCOL, 128), 1)
     taper = 0.5 - 0.5 * jnp.cos(2.0 * math.pi * (when.astype(F32) + 0.5) / TIME)
     pad[:, :PAD, :] = jnp.zeros((3, PAD, 128), F32)
     pad[:, PAD + TIME :, :] = jnp.zeros((3, PAD, 128), F32)
     everyone = pltpu.make_async_remote_copy(
-        src_ref=stage.at[0 : NDEV - 1],
-        dst_ref=land.at[0 : NDEV - 1],
+        src_ref=stage.at[0 : NCHIP - 1],
+        dst_ref=mid.at[0 : NCHIP - 1],
         send_sem=ss,
         recv_sem=rs,
-        device_id=(r, c),
+        device_id=across,
         device_id_type=MESH,
     )
     everyone.wait_recv()
+    swap = pltpu.make_async_remote_copy(
+        src_ref=mid.at[:, 1 - core],
+        dst_ref=land.at[:, core],
+        send_sem=sx,
+        recv_sem=rx,
+        device_id=across,
+        device_id_type=MESH,
+    )
+    swap.start()
+    land[:, pl.ds(core, 1)] = mid[:, pl.ds(core, 1)]
+    swap.wait_recv()
 
     down = lax.broadcasted_iota(jnp.int32, (DAYS, 128), 0).astype(F32)
     for k in range(NCOL):
-        here = land[8 * k : 8 * k + 8].reshape(128, 128).astype(F32).T
+        here = land[4 * k : 4 * k + 4].reshape(128, 128).astype(F32).T
         lanes = slice(k * 128, (k + 1) * 128)
         xt[:, lanes] = here[: 2 * OWN]
         day_row = here[96:97] * 256.0 + here[97:98]
@@ -196,7 +214,6 @@
             at[pl.ds(pl.multiple_of(c * OWN, 16), OWN), lanes] = anomaly[:OWN]
             bt[pl.ds(pl.multiple_of(r * OWN, 16), OWN), lanes] = anomaly[OWN:]
 
-    core = lax.rem(c, 2)
     ring_a = Ring(
         at,
         lambda p, q: p * 8 + q * 2 + core,
@@ -226,7 +243,7 @@
             dst_ref=ref,
             send_sem=ssib.at[j, n],
             recv_sem=rsib.at[j, n],
-            device_id=(r, c + 1 - 2 * core),
+            device_id=across,
             device_id_type=MESH,
         )
         copy.start()
@@ -284,47 +301,35 @@
             now, later = (even, odd) if pair % 2 == 0 else (odd, even)
             if pair + 1 < PAIRS:
                 fill(pad, held_lags[2 * pair + 2 + m], m, first, WINDOW, later)
-            prod = dot(at[m * 384 : (m + 1) * 384, first : first + WINDOW], now[...])
-            for i in range(2):
-                where = (2 * pair + i, slice(m * 384, (m + 1) * 384))
-                here = prod[:, i * COLW : (i + 1) * COLW]
-                part[where] = here if j == 0 else part[where] + here
+            rows = slice(m * 384, (m + 1) * 384)
+            part[pair, rows] = dot(at[rows, first : first + WINDOW], now[...])
             for act in between.get(n, ()):
                 act()
 
-    for j in range(4):
-        ring_a.across(j)
-        ring_b.across(j)
+    ring_a.across(0)
+    ring_b.across(0)
     own(0)
+    ring_a.across(1)
+    ring_b.across(1)
+    near(0)
     own(1)
-    near(0)
     other(0)
-    own(2)
-    near(1)
     far(0)
-    own(3)
-    other(1)
     last(0)
     turn(0)
     close(0)
     products(
         0,
         {
-            0: [lambda: near(2)],
-            2: [lambda: far(1)],
-            3: [lambda: other(2)],
-            5: [lambda: near(3)],
+            0: [lambda: near(1)],
+            2: [lambda: other(1)],
+            4: [lambda: far(1)],
             6: [lambda: last(1)],
         },
     )
     turn(1)
     close(1)
-    products(1, {1: [lambda: far(2)], 3: [lambda: other(3)], 5: [lambda: last(2)]})
-    turn(2)
-    close(2)
-    products(2, {2: [lambda: far(3)], 6: [lambda: last(3)]})
-    turn(3)
-    close(3)
+    swap.wait_send()
     everyone.wait_send()
     for copy in list(siblings.values()) + list(ring_a.copies.values()) + list(ring_b.copies.values()):
         copy.wait_send()
@@ -340,7 +345,7 @@
             jax.ShapeDtypeStruct((ROWW, TIME), BF16),
             jax.ShapeDtypeStruct((3, TIME + 2 * PAD, 128), F32),
             jax.ShapeDtypeStruct((NLAG, 128), F32),
-            jax.ShapeDtypeStruct((NLAG, ROWW, COLW), F32),
+            jax.ShapeDtypeStruct((PAIRS, ROWW, 2 * COLW), F32),
         ),
         in_specs=[hbm, hbm, hbm],
         out_specs=(vmem, vmem, vmem, vmem),
@@ -348,8 +353,9 @@
             pltpu.VMEM((STEPS, CHANS), BF16),
             pltpu.SMEM((STEPS,), jnp.int32),
             pltpu.SMEM((NLAG,), jnp.int32),
-            pltpu.VMEM((NDEV, STEPS, 128), BF16),
-            pltpu.VMEM((NDEV, STEPS, 128), BF16),
+            pltpu.VMEM((NCHIP, 2, STEPS, 128), BF16),
+            pltpu.VMEM((NCHIP, 2, STEPS, 128), BF16),
+            pltpu.VMEM((NCHIP, 2, STEPS, 128), BF16),
             pltpu.VMEM((2 * OWN, TIME), F32),
             pltpu.VMEM((DAYS, TIME), BF16),
             pltpu.VMEM((COLW, TIME), BF16),
@@ -358,12 +364,14 @@
             dma((3,)),
             dma(()),
             dma(()),
-            dma((4, 9)),
-            dma((4, 9)),
-            dma((4, 9)),
-            dma((4, 9)),
-            dma((4, 8)),
-            dma((4, 8)),
+            dma(()),
+            dma(()),
+            dma((2, 9)),
+            dma((2, 9)),
+            dma((2, 9)),
+            dma((2, 9)),
+            dma((2, 8)),
+            dma((2, 8)),
         ],
         compiler_params=pltpu.CompilerParams(
             collective_id=0, has_side_effects=True, vmem_limit_bytes=24 * 2**20
@@ -372,55 +380,45 @@
     )(*(pltpu.with_memory_space_constraint(x, pltpu.HBM) for x in (series, day_index, lags)))
 
 
-def cov_kernel(at, pad, lagv, part, out, even, odd):
+def cov_kernel(at, pad, lagv, part, out, even, odd, done, sems):
     first = TIME - WINDOW
-    g = pl.program_id(0)
-    m = pl.program_id(1)
-
-    def shift(pair, i, held):
-        lag = jnp.max(lagv[pl.ds(2 * pair + i, 1), :]).astype(jnp.int32)
-        fill(pad, lag, i, first, WINDOW, held)
-
-    @pl.when((g == 0) & (m == 0))
-    def _():
-        shift(0, 0, even)
-        shift(0, 1, even)
-
-    def body(now, later):
+    lag = [jnp.max(lagv[k : k + 1, :]).astype(jnp.int32) for k in range(NLAG)]
+    for i in range(2):
+        fill(pad, lag[i], i, first, WINDOW, even)
+    copies = []
+    for n in range(2 * PAIRS):
+        pair, m = n // 2, n % 2
+        now, later = (even, odd) if pair % 2 == 0 else (odd, even)
+        slot = n % SLOTS
+        if n >= SLOTS:
+            copies[n - SLOTS].wait()
+        if pair + 1 < PAIRS:
+            fill(pad, lag[2 * pair + 2 + m], m, first, WINDOW, later)
+        rows = slice(m * 384, (m + 1) * 384)
+        total = (part[pair, rows] + dot(at[rows, first:], now[...])) * (1.0 / TIME)
         for i in range(2):
-
-            @pl.when(m == i)
-            def _():
-                shift(lax.rem(g + 1, PAIRS), i, later)
-                rows = slice(i * 384, (i + 1) * 384)
-                prod = dot(at[rows, first:], now[...])
-                out[0] = (part[2 * g, rows] + prod[:, :COLW]) * (1.0 / TIME)
-                out[1] = (part[2 * g + 1, rows] + prod[:, COLW:]) * (1.0 / TIME)
-
-    @pl.when(lax.rem(g, 2) == 0)
-    def _():
-        body(even, odd)
-
-    @pl.when(lax.rem(g, 2) == 1)
-    def _():
-        body(odd, even)
+            done[slot, i] = total[:, i * COLW : (i + 1) * COLW]
+        copy = pltpu.make_async_copy(done.at[slot], out.at[2 * pair : 2 * pair + 2, rows], sems.at[slot])
+        copy.start()
+        copies.append(copy)
+    for copy in copies[-SLOTS:]:
+        copy.wait()
 
 
 def covariance(at, pad, lagv, part):
     vmem = pl.BlockSpec(memory_space=pltpu.VMEM)
     return pl.pallas_call(
         cov_kernel,
-        grid=(PAIRS, 2),
         out_shape=jax.ShapeDtypeStruct((NLAG, ROWW, COLW), F32),
         in_specs=[vmem] * 4,
-        out_specs=pl.BlockSpec((2, ROWW // 2, COLW), lambda g, m: (g, m, 0)),
+        out_specs=pl.BlockSpec(memory_space=pltpu.HBM),
         scratch_shapes=[
             pltpu.VMEM((WINDOW, 2 * COLW), BF16),
             pltpu.VMEM((WINDOW, 2 * COLW), BF16),
+            pltpu.VMEM((SLOTS, 2, 384, COLW), F32),
+            pltpu.SemaphoreType.DMA((SLOTS,)),
         ],
-        compiler_params=pltpu.CompilerParams(
-            dimension_semantics=("arbitrary", "arbitrary"), vmem_limit_bytes=20 * 2**20
-        ),
+        compiler_params=pltpu.CompilerParams(vmem_limit_bytes=20 * 2**20),
         name="lagged_covariance",
     )(at, pad, lagv, part)
 

time: 62.8 us -> 61.2 us (0.975)
  Pallas kernels: 62.7 us -> 61.1 us
    pallas_call x1, Pallas kernels: 55.7 us -> 52.2 us  [gather(): pl.pallas_call(gather_kernel, out_shape=(jax.ShapeDtypeStruct((ROWW, TIME...]
    pallas_call x1, Pallas kernels: 6.98 us -> 8.94 us  [covariance(): pl.pallas_call(cov_kernel, out_shape=jax.ShapeDtypeStruct((NLAG, ROWW, CO...]
where the time goes in v3:
time: 61.2 us; the launch traced here: 61.1 us
  Pallas kernels  61.1 us (100%)
    pallas_call x1, Pallas kernels, gather(): pl.pallas_call(gather_kernel, out_shape=(jax.ShapeDtypeStruct((ROWW, TIME...  52.2 us
    pallas_call x1, Pallas kernels, covariance(): pl.pallas_call(cov_kernel, out_shape=jax.ShapeDtypeStruct((NLAG, ROWW, CO...  8.94 us

profile of v3, /device:TPU:1, one launch (start us, length us, event | category | flops | bytes accessed | tf_op | source)
XLA Modules:
  0.0 61.1 jit_solution(848916194221650299)
XLA Ops:
  0.0 52.2 %gather_anomaly.1 = (bf16[768,2048]{1,0:T(8,128)(2,1)S(1)}, f32[3,2112,128]{2,1,0:T(8,128)S(1)}, f32[8,128]{1,0:T(8,128)S(1)}, f32[4,768,768]{2,1,0:T(8,128)S(1)}) custom-call(bf16[16,6144]{1,0:T(8,128)(2,1)} %series.1, s32[16]{0:T(128)} %days.1, s32[8]{0:T(128)} %lags.1), custom_call_target="tpu_custom_call" | custom-call | tf_op jit(solution)/shard_map/gather_anomaly/pallas_call | solution.py:342
  52.2 8.9 %lagged_covariance.1 = f32[8,768,384]{2,1,0:T(8,128)} custom-call(bf16[768,2048]{1,0:T(8,128)(2,1)S(1)} %get-tuple-element.9.at, f32[3,2112,128]{2,1,0:T(8,128)S(1)} %get-tuple-element.10.pad, f32[8,128]{1,0:T(8,128)S(1)} %get-tuple-element.11.lagv, f32[4,768,768]{2,1,0:T(8,128)S(1)} %get-tuple-element.12.part), custom_call_target="tpu_custom_call" | custom-call | tf_op jit(solution)/shard_map/lagged_covariance/pallas_call | solution.py:410

commit v4 on v1

v4 whole, which is shorter than its diff:
```python
import math

import jax
import jax.numpy as jnp
from jax import lax
from jax.experimental import pallas as pl
from jax.experimental.pallas import tpu as pltpu
from jax.sharding import PartitionSpec as P

NLAG = 8
DAYS = 384
TIME = 2048
NROW = 8
NCOL = 16
STEPS = 16
ROWW = 768
COLW = 384
EXT = ROWW + 16
PAD = 32
CHANS = 6144
GROUP = 4
NPART = 4
PART = ROWW // NPART
SLOTS = 3
MESH = pl.DeviceIdType.MESH
F32 = jnp.float32
BF16 = jnp.bfloat16


class Ring:
    def __init__(self, view, half, slot, device, p, q, send, recv):
        self.view, self.half, self.slot, self.device = view, half, slot, device
        self.p, self.q, self.send, self.recv = p, q, send, recv
        self.copies = {}

    def at(self, dq):
        return lax.rem(self.q + dq + 4, 4)

    def copy(self, n, ref, dev):
        copy = pltpu.make_async_remote_copy(
            src_ref=ref,
            dst_ref=ref,
            send_sem=self.send.at[n],
            recv_sem=self.recv.at[n],
            device_id=dev,
            device_id_type=MESH,
        )
        copy.start()
        self.copies[n] = copy

    def own(self):
        ref = self.view(self.slot(self.p, self.q))
        self.copy(1, ref, self.device(self.p, self.at(1)))
        self.copy(2, ref, self.device(self.p, self.at(-1)))
        self.copy(0, ref, self.device(1 - self.p, self.q))

    def other(self):
        self.copies[0].wait_recv()
        ref = self.view(self.slot(1 - self.p, self.q))
        self.copy(3, ref, self.device(self.p, self.at(1)))
        self.copy(4, ref, self.device(self.p, self.at(-1)))

    def forward(self, n):
        self.copies[n].wait_recv()
        pair = self.p if n < 3 else 1 - self.p
        if n % 2 == 1:
            ref = self.half(self.slot(pair, self.at(-1)), 0)
            self.copy(n + 4, ref, self.device(self.p, self.at(1)))
        else:
            ref = self.half(self.slot(pair, self.at(1)), 1)
            self.copy(n + 4, ref, self.device(self.p, self.at(-1)))


def gather_kernel(
    series, days, lags, at, bp, lagv,
    held, held_days, held_lags, stage, land, sl, sa, ra, sb, rb, sra, rra, srb, rrb, ssib, rsib,
):
    r = lax.axis_index("row")
    c = lax.axis_index("col")
    loads = [
        pltpu.make_async_copy(series, held, sl.at[0]),
        pltpu.make_async_copy(days, held_days, sl.at[1]),
        pltpu.make_async_copy(lags, held_lags, sl.at[2]),
    ]
    for load in loads:
        load.start()
    barrier = pltpu.get_barrier_semaphore()
    for j in range(1, NROW):
        pl.semaphore_signal(barrier, inc=1, device_id=(lax.rem(r + j, NROW), c), device_id_type=MESH)
    for j in range(1, NCOL):
        pl.semaphore_signal(barrier, inc=1, device_id=(r, lax.rem(c + j, NCOL)), device_id_type=MESH)

    for load in loads:
        load.wait()
    step = lax.broadcasted_iota(jnp.int32, (STEPS, 128), 0)
    lane = lax.broadcasted_iota(jnp.int32, (STEPS, 128), 1)
    day = jnp.zeros((STEPS, 128), jnp.int32)
    for i in range(STEPS):
        day = jnp.where(step == i, held_days[i], day)
    high = jnp.right_shift(day, 8)
    info = jnp.where(lane == 0, high, jnp.where(lane == 1, day - high * 256, 0))
    info = info.astype(F32).astype(BF16)
    for d in range(NROW):
        stage[d, :, :ROWW] = held[:, d * ROWW : (d + 1) * ROWW]
        stage[d, :, ROWW:] = info

    for k in range(NLAG):
        lagv[k : k + 1, :] = jnp.full((1, 128), held_lags[k], jnp.int32).astype(F32)
    pl.semaphore_wait(barrier, NROW + NCOL - 2)

    rows, cols = [], []
    for j in range(1, NROW):
        to = lax.rem(r + j, NROW)
        copy = pltpu.make_async_remote_copy(
            src_ref=stage.at[to],
            dst_ref=land.at[r],
            send_sem=sa.at[j],
            recv_sem=ra.at[j],
            device_id=(to, c),
            device_id_type=MESH,
        )
        copy.start()
        rows.append(copy)
    for j in range(1, NCOL):
        to = lax.rem(c + j, NCOL)
        copy = pltpu.make_async_remote_copy(
            src_ref=held.at[:, pl.ds(pl.multiple_of(to * COLW, 128), COLW)],
            dst_ref=bp.at[c, r],
            send_sem=sb.at[j],
            recv_sem=rb.at[j],
            device_id=(r, to),
            device_id_type=MESH,
        )
        copy.start()
        cols.append(copy)
    land[r] = stage[r]
    bp[c, r] = held[:, pl.ds(pl.multiple_of(c * COLW, 128), COLW)]

    core = lax.rem(c, 2)
    ring_a = Ring(
        lambda s: at.at[s],
        lambda s, h: at.at[s, 400 * h : 400 + 384 * h],
        lambda p, q: p * 8 + q * 2 + core,
        lambda p, q: (r, p * 8 + q * 2 + core),
        c // 8,
        lax.rem(c // 2, 4),
        sra,
        rra,
    )
    ring_b = Ring(
        lambda s: bp.at[:, s],
        lambda s, h: bp.at[8 * h : 8 * h + 8, s],
        lambda p, q: p * 4 + q,
        lambda p, q: (p * 4 + q, c),
        r // 4,
        lax.rem(r, 4),
        srb,
        rrb,
    )
    siblings = []

    def sibling(p, q):
        n = len(siblings)
        ref = at.at[ring_a.slot(p, q)]
        copy = pltpu.make_async_remote_copy(
            src_ref=ref,
            dst_ref=ref,
            send_sem=ssib.at[n],
            recv_sem=rsib.at[n],
            device_id=(r, c + 1 - 2 * core),
            device_id_type=MESH,
        )
        copy.start()
        siblings.append(copy)

    for copy in rows:
        copy.wait_recv()
    block = land[...].reshape(NROW * STEPS, ROWW + 128).astype(F32)
    at[c] = block.T[:EXT].astype(BF16)
    ring_a.own()
    for copy in cols:
        copy.wait_recv()
    ring_b.own()
    pa, qa = ring_a.p, ring_a.q
    sibling(pa, qa)
    ring_a.other()
    ring_b.other()
    ring_a.forward(1)
    ring_a.forward(2)
    ring_b.forward(1)
    ring_b.forward(2)
    sibling(1 - pa, qa)
    sibling(pa, ring_a.at(-1))
    sibling(pa, ring_a.at(1))
    ring_a.forward(3)
    ring_a.forward(4)
    ring_b.forward(3)
    ring_b.forward(4)
    sibling(1 - pa, ring_a.at(-1))
    sibling(1 - pa, ring_a.at(1))
    for pair, first in ((pa, 5), (1 - pa, 7)):
        ring_a.copies[first].wait_recv()
        ring_a.copies[first + 1].wait_recv()
        sibling(pair, ring_a.at(2))
    for n in (5, 6, 7, 8):
        ring_b.copies[n].wait_recv()
    for copy in siblings:
        copy.wait()
    for copy in rows + cols + list(ring_a.copies.values()) + list(ring_b.copies.values()):
        copy.wait_send()


def hbm(x):
    return pltpu.with_memory_space_constraint(x, pltpu.HBM)


HBM = pl.BlockSpec(memory_space=pltpu.HBM)
VMEM = pl.BlockSpec(memory_space=pltpu.VMEM)
DMA = pltpu.SemaphoreType.DMA


def gather(series, day_index, lags):
    return pl.pallas_call(
        gather_kernel,
        out_shape=(
            jax.ShapeDtypeStruct((NCOL, EXT, 128), BF16),
            jax.ShapeDtypeStruct((NCOL, NROW, STEPS, COLW), BF16),
            jax.ShapeDtypeStruct((NLAG, 128), F32),
        ),
        in_specs=[HBM, HBM, HBM],
        out_specs=(VMEM, VMEM, VMEM),
        scratch_shapes=[
            pltpu.VMEM((STEPS, CHANS), BF16),
            pltpu.SMEM((STEPS,), jnp.int32),
            pltpu.SMEM((NLAG,), jnp.int32),
            pltpu.VMEM((NROW, STEPS, ROWW + 128), BF16),
            pltpu.VMEM((NROW, STEPS, ROWW + 128), BF16),
            DMA((3,)),
            DMA((NROW,)),
            DMA((NROW,)),
            DMA((NCOL,)),
            DMA((NCOL,)),
            DMA((9,)),
            DMA((9,)),
            DMA((9,)),
            DMA((9,)),
            DMA((8,)),
            DMA((8,)),
        ],
        compiler_params=pltpu.CompilerParams(
            collective_id=0, has_side_effects=True, vmem_limit_bytes=8 * 2**20
        ),
        name="gather_series",
    )(hbm(series), hbm(day_index), hbm(lags))


def fill(pad, lag, i, held):
    for k in range(NCOL):
        for b in range(NROW):
            to = (k * NROW + b) * 16
            for w in range(3):
                piece = pad[w, pl.ds(PAD + b * 256 + k * 16 + lag, 16), :]
                held[to : to + 16, i * COLW + w * 128 : i * COLW + (w + 1) * 128] = piece.astype(BF16)


def dot(a, b):
    return jnp.dot(a, b, preferred_element_type=F32)


def split(x):
    high = x.astype(BF16)
    return high, (x - high.astype(F32)).astype(BF16)


def cov_kernel(lagv, at, bp, out, anom, onehot, onehot_t, pad, early, late, done, sems):
    lag = [jnp.max(lagv[k : k + 1, :]).astype(jnp.int32) for k in range(NLAG)]
    place = lax.broadcasted_iota(jnp.int32, (NCOL, 128), 1)
    when = place // STEPS * (NCOL * STEPS) + lax.broadcasted_iota(jnp.int32, (NCOL, 128), 0) * STEPS + place % STEPS
    taper = 0.5 - 0.5 * jnp.cos(2.0 * math.pi * (when.astype(F32) + 0.5) / TIME)
    taper_t = taper.T

    info = at[:, ROWW:, :].astype(F32)
    day = info[:, 0, :] * 256.0 + info[:, 1, :]
    day_t = day.T
    down = lax.broadcasted_iota(jnp.int32, (DAYS, 128), 0).astype(F32)
    along = lax.broadcasted_iota(jnp.int32, (128, DAYS), 1).astype(F32)
    count = jnp.zeros((DAYS, 128), F32)
    for k in range(NCOL):
        steps = slice(k * 128, (k + 1) * 128)
        here = jnp.where(down == day[k : k + 1, :], 1.0, 0.0)
        count = count + here
        hot = here.astype(BF16)
        onehot[:DAYS, steps] = hot
        onehot[DAYS:, steps] = hot
        hot = jnp.where(along == day_t[:, k : k + 1], 1.0, 0.0).astype(BF16)
        onehot_t[steps, :DAYS] = hot
        onehot_t[steps, DAYS:] = hot
    inv_col = 1.0 / jnp.maximum(jnp.sum(count, axis=1, keepdims=True), 1.0)
    inv_row = jnp.broadcast_to(inv_col, (DAYS, 128)).T[0:1, :]

    sums = dot(onehot[:DAYS, :], bp[...].reshape(TIME, COLW))
    both = jnp.concatenate(split(sums * inv_col), axis=0)
    pad[:, :PAD, :] = jnp.zeros((3, PAD, 128), F32)
    pad[:, PAD + TIME :, :] = jnp.zeros((3, PAD, 128), F32)
    for q in range(4):
        season = dot(onehot_t[q * 512 : (q + 1) * 512, :], both)
        for k in range(4 * q, 4 * q + 4):
            here = bp[k].reshape(128, COLW).astype(F32) - season[(k - 4 * q) * 128 : (k - 4 * q + 1) * 128]
            here = (here * taper_t[:, k : k + 1]).astype(BF16).astype(F32)
            for b in range(NROW):
                row = PAD + b * 256 + k * 16
                for w in range(3):
                    pad[w, row : row + 16, :] = here[b * 16 : (b + 1) * 16, w * 128 : (w + 1) * 128]

    for m in range(3):
        rows = slice(m * 256, (m + 1) * 256)
        block = jnp.concatenate([at[k, rows, :] for k in range(NCOL)], axis=1)
        sums = lax.dot_general(block, onehot[:DAYS, :], (((1,), (1,)), ((), ())), preferred_element_type=F32)
        both = jnp.concatenate(split(sums * inv_row), axis=1)
        for k in range(GROUP):
            if k % 3 == m:
                fill(pad, lag[k], k, early)
        for n in range(2):
            season = dot(both, onehot[:, n * 1024 : (n + 1) * 1024])
            for i in range(8):
                k = 8 * n + i
                here = at[k, rows, :].astype(F32) - season[:, i * 128 : (i + 1) * 128]
                anom[rows, k * 128 : (k + 1) * 128] = (here * taper[k : k + 1, :]).astype(BF16)

    copies = []
    for n in range(2 * NPART):
        group, m = divmod(n, NPART)
        slot = n % SLOTS
        if n >= SLOTS:
            copies[n - SLOTS].wait()
        if group == 0:
            fill(pad, lag[GROUP + m], m, late)
        rows = slice(m * PART, (m + 1) * PART)
        total = dot(anom[rows, :], (early if group == 0 else late)[...]) * (1.0 / TIME)
        for i in range(GROUP):
            done[slot, i] = total[:, i * COLW : (i + 1) * COLW]
        copy = pltpu.make_async_copy(done.at[slot], out.at[group * GROUP : (group + 1) * GROUP, rows], sems.at[slot])
        copy.start()
        copies.append(copy)
    for copy in copies[-SLOTS:]:
        copy.wait()


def covariance(at, bp, lagv):
    return pl.pallas_call(
        cov_kernel,
        out_shape=jax.ShapeDtypeStruct((NLAG, ROWW, COLW), F32),
        in_specs=[VMEM] * 3,
        out_specs=HBM,
        scratch_shapes=[
            pltpu.VMEM((ROWW, TIME), BF16),
            pltpu.VMEM((2 * DAYS, TIME), BF16),
            pltpu.VMEM((TIME, 2 * DAYS), BF16),
            pltpu.VMEM((3, TIME + 2 * PAD, 128), F32),
            pltpu.VMEM((TIME, GROUP * COLW), BF16),
            pltpu.VMEM((TIME, GROUP * COLW), BF16),
            pltpu.VMEM((SLOTS, GROUP, PART, COLW), F32),
            DMA((SLOTS,)),
        ],
        compiler_params=pltpu.CompilerParams(vmem_limit_bytes=48 * 2**20),
        name="lagged_covariance",
    )(lagv, at, bp)


def shards(series, day_index, lags):
    return covariance(*gather(series, day_index, lags))


def solution(mesh):
    placed = (P(("row", "col"), None), P(("row", "col")), P())
    return jax.shard_map(
        shards, mesh=mesh, in_specs=placed, out_specs=P(None, "row", "col"), check_vma=False
    )
```

time: 63.7 us -> 56.2 us (0.88)
  Pallas kernels: 61.3 us -> 55.7 us
  local copies, waits for them, and re-layouts: 2.24 us -> 0 us
    pallas_call x2, Pallas kernels: 61.3 us -> 55.7 us  [the longest x1 34.9 us: gather(): pl.pallas_call(gather_kernel, out_shape=(jax.ShapeDtypeStruct((NCOL, EXT,...]
    unnamed x6 -> x0, local copies, waits for them, and re-layouts: 2.24 us -> none
where the time goes in v4:
time: 56.2 us; the launch traced here: 55.8 us
  Pallas kernels  55.7 us (99%)
    pallas_call x1, Pallas kernels, gather(): pl.pallas_call(gather_kernel, out_shape=(jax.ShapeDtypeStruct((NCOL, EXT,...  34.9 us
    pallas_call x1, Pallas kernels, covariance(): pl.pallas_call(cov_kernel, out_shape=jax.ShapeDtypeStruct((NLAG, ROWW, CO...  20.8 us

profile of v4, /device:TPU:1, one launch (start us, length us, event | category | flops | bytes accessed | tf_op | source)
XLA Modules:
  0.0 55.8 jit_solution(3717070084664459455)
XLA Ops:
  0.0 34.9 %gather_series.1 = (bf16[16,784,128]{2,1,0:T(8,128)(2,1)S(1)}, bf16[16,8,16,384]{3,2,1,0:T(8,128)(2,1)S(1)}, f32[8,128]{1,0:T(8,128)S(1)}) custom-call(bf16[16,6144]{1,0:T(8,128)(2,1)} %series.1, s32[16]{0:T(128)} %days.1, s32[8]{0:T(128)} %lags.1), custom_call_target="tpu_custom_call" | custom-call | tf_op jit(solution)/shard_map/gather_series/pallas_call | solution.py:223
  34.9 20.8 %lagged_covariance.1 = f32[8,768,384]{2,1,0:T(8,128)} custom-call(f32[8,128]{1,0:T(8,128)S(1)} %get-tuple-element.8.lagv, bf16[16,784,128]{2,1,0:T(8,128)(2,1)S(1)} %get-tuple-element.9.at, bf16[16,8,16,384]{3,2,1,0:T(8,128)(2,1)S(1)} %get-tuple-element.10.bp), custom_call_target="tpu_custom_call" | custom-call | tf_op jit(solution)/shard_map/lagged_covariance/pallas_call | solution.py:350

commit v5 on v4

--- a/solution.py
+++ b/solution.py
@@ -19,7 +19,7 @@
 PAD = 32
 CHANS = 6144
 GROUP = 4
-NPART = 4
+NPART = 2
 PART = ROWW // NPART
 SLOTS = 3
 MESH = pl.DeviceIdType.MESH
@@ -287,6 +287,7 @@
     count = jnp.zeros((DAYS, 128), F32)
     for k in range(NCOL):
         steps = slice(k * 128, (k + 1) * 128)
+        anom[:, steps] = at[k, :ROWW, :]
         here = jnp.where(down == day[k : k + 1, :], 1.0, 0.0)
         count = count + here
         hot = here.astype(BF16)
@@ -312,20 +313,15 @@
                 for w in range(3):
                     pad[w, row : row + 16, :] = here[b * 16 : (b + 1) * 16, w * 128 : (w + 1) * 128]
 
-    for m in range(3):
-        rows = slice(m * 256, (m + 1) * 256)
-        block = jnp.concatenate([at[k, rows, :] for k in range(NCOL)], axis=1)
-        sums = lax.dot_general(block, onehot[:DAYS, :], (((1,), (1,)), ((), ())), preferred_element_type=F32)
-        both = jnp.concatenate(split(sums * inv_row), axis=1)
-        for k in range(GROUP):
-            if k % 3 == m:
-                fill(pad, lag[k], k, early)
-        for n in range(2):
-            season = dot(both, onehot[:, n * 1024 : (n + 1) * 1024])
-            for i in range(8):
-                k = 8 * n + i
-                here = at[k, rows, :].astype(F32) - season[:, i * 128 : (i + 1) * 128]
-                anom[rows, k * 128 : (k + 1) * 128] = (here * taper[k : k + 1, :]).astype(BF16)
+    sums = lax.dot_general(anom[...], onehot[:DAYS, :], (((1,), (1,)), ((), ())), preferred_element_type=F32)
+    both = jnp.concatenate(split(sums * inv_row), axis=1)
+    for n in range(4):
+        fill(pad, lag[n], n, early)
+        season = dot(both, onehot[:, n * 512 : (n + 1) * 512])
+        for k in range(4 * n, 4 * n + 4):
+            steps = slice(k * 128, (k + 1) * 128)
+            here = anom[:, steps].astype(F32) - season[:, (k - 4 * n) * 128 : (k - 4 * n + 1) * 128]
+            anom[:, steps] = (here * taper[k : k + 1, :]).astype(BF16)
 
     copies = []
     for n in range(2 * NPART):
@@ -334,7 +330,8 @@
         if n >= SLOTS:
             copies[n - SLOTS].wait()
         if group == 0:
-            fill(pad, lag[GROUP + m], m, late)
+            for k in range(m * GROUP // NPART, (m + 1) * GROUP // NPART):
+                fill(pad, lag[GROUP + k], k, late)
         rows = slice(m * PART, (m + 1) * PART)
         total = dot(anom[rows, :], (early if group == 0 else late)[...]) * (1.0 / TIME)
         for i in range(GROUP):

time: 56.2 us -> 54.8 us (0.975)
  Pallas kernels: 55.7 us -> 54.3 us
    pallas_call x1, Pallas kernels: 20.8 us -> 19.4 us  [covariance(): pl.pallas_call(cov_kernel, out_shape=jax.ShapeDtypeStruct((NLAG, ROWW, CO...]
where the time goes in v5:
time: 54.8 us; the launch traced here: 54.4 us
  Pallas kernels  54.3 us (99%)
    pallas_call x1, Pallas kernels, gather(): pl.pallas_call(gather_kernel, out_shape=(jax.ShapeDtypeStruct((NCOL, EXT,...  34.9 us
    pallas_call x1, Pallas kernels, covariance(): pl.pallas_call(cov_kernel, out_shape=jax.ShapeDtypeStruct((NLAG, ROWW, CO...  19.4 us

profile of v5, /device:TPU:1, one launch (start us, length us, event | category | flops | bytes accessed | tf_op | source)
XLA Modules:
  0.0 54.4 jit_solution(7287765249367298045)
XLA Ops:
  0.0 34.9 %gather_series.1 = (bf16[16,784,128]{2,1,0:T(8,128)(2,1)S(1)}, bf16[16,8,16,384]{3,2,1,0:T(8,128)(2,1)S(1)}, f32[8,128]{1,0:T(8,128)S(1)}) custom-call(bf16[16,6144]{1,0:T(8,128)(2,1)} %series.1, s32[16]{0:T(128)} %days.1, s32[8]{0:T(128)} %lags.1), custom_call_target="tpu_custom_call" | custom-call | tf_op jit(solution)/shard_map/gather_series/pallas_call | solution.py:223
  34.9 19.4 %lagged_covariance.1 = f32[8,768,384]{2,1,0:T(8,128)} custom-call(f32[8,128]{1,0:T(8,128)S(1)} %get-tuple-element.8.lagv, bf16[16,784,128]{2,1,0:T(8,128)(2,1)S(1)} %get-tuple-element.9.at, bf16[16,8,16,384]{3,2,1,0:T(8,128)(2,1)S(1)} %get-tuple-element.10.bp), custom_call_target="tpu_custom_call" | custom-call | tf_op jit(solution)/shard_map/lagged_covariance/pallas_call | solution.py:347

commit v6 on v5

v6 whole, which is shorter than its diff:
```python
import math

import jax
import jax.numpy as jnp
from jax import lax
from jax.experimental import pallas as pl
from jax.experimental.pallas import tpu as pltpu
from jax.sharding import PartitionSpec as P

NLAG = 8
DAYS = 384
TIME = 2048
NROW = 8
NCOL = 16
STEPS = 16
ROWW = 768
COLW = 384
EXT = ROWW + 16
PAD = 32
INFO = 16
HALF = ROWW // 2
COLS = (0, 256, 384)
ROWS = (0, INFO + HALF, EXT)
MIDS = (208, 592)
CHANS = 6144
GROUP = 4
SLOTS = 2
MESH = pl.DeviceIdType.MESH
F32 = jnp.float32
BF16 = jnp.bfloat16


class Ring:
    def __init__(self, view, half, slot, device, p, q, send, recv):
        self.view, self.half, self.slot, self.device = view, half, slot, device
        self.p, self.q, self.send, self.recv = p, q, send, recv
        self.copies = {}

    def at(self, dq):
        return lax.rem(self.q + dq + 4, 4)

    def copy(self, j, n, ref, dev):
        copy = pltpu.make_async_remote_copy(
            src_ref=ref,
            dst_ref=ref,
            send_sem=self.send.at[j, n],
            recv_sem=self.recv.at[j, n],
            device_id=dev,
            device_id_type=MESH,
        )
        copy.start()
        self.copies[j, n] = copy

    def own(self, j):
        ref = self.view(self.slot(self.p, self.q), j)
        self.copy(j, 0, ref, self.device(1 - self.p, self.q))
        self.copy(j, 1, ref, self.device(self.p, self.at(1)))
        self.copy(j, 2, ref, self.device(self.p, self.at(-1)))

    def other(self, j):
        self.copies[j, 0].wait_recv()
        ref = self.view(self.slot(1 - self.p, self.q), j)
        self.copy(j, 3, ref, self.device(self.p, self.at(1)))
        self.copy(j, 4, ref, self.device(self.p, self.at(-1)))

    def forward(self, j, n):
        self.copies[j, n].wait_recv()
        pair = self.p if n < 3 else 1 - self.p
        if n % 2 == 1:
            self.copy(j, n + 4, self.half(self.slot(pair, self.at(-1)), j, 0), self.device(self.p, self.at(1)))
        else:
            self.copy(j, n + 4, self.half(self.slot(pair, self.at(1)), j, 1), self.device(self.p, self.at(-1)))


def dot(a, b):
    return jnp.dot(a, b, preferred_element_type=F32)


def split(x):
    high = x.astype(BF16)
    return high, (x - high.astype(F32)).astype(BF16)


def taper_of():
    place = lax.broadcasted_iota(jnp.int32, (NCOL, 128), 1)
    when = place // STEPS * (NCOL * STEPS) + lax.broadcasted_iota(jnp.int32, (NCOL, 128), 0) * STEPS + place % STEPS
    return 0.5 - 0.5 * jnp.cos(2.0 * math.pi * (when.astype(F32) + 0.5) / TIME)


def column_part(bp, j, onehot, onehot_t, inv_col, taper_t, pad):
    lanes = slice(COLS[j], COLS[j + 1])
    width = COLS[j + 1] - COLS[j]
    sums = dot(onehot[:DAYS, :], bp[:, :, :, lanes].reshape(TIME, width))
    both = jnp.concatenate(split(sums * inv_col), axis=0)
    pad[:, :PAD, :] = jnp.zeros((width // 128, PAD, 128), F32)
    pad[:, PAD + TIME :, :] = jnp.zeros((width // 128, PAD, 128), F32)
    for q in range(4):
        season = dot(onehot_t[q * 512 : (q + 1) * 512, :], both)
        for k in range(4 * q, 4 * q + 4):
            here = bp[k, :, :, lanes].reshape(128, width).astype(F32) - season[(k - 4 * q) * 128 : (k - 4 * q + 1) * 128]
            here = (here * taper_t[:, k : k + 1]).astype(BF16).astype(F32)
            for b in range(NROW):
                row = PAD + b * 256 + k * 16
                for w in range(width // 128):
                    pad[w, row : row + 16, :] = here[b * 16 : (b + 1) * 16, w * 128 : (w + 1) * 128]


def row_sums(at, j, onehot, inv_row, anom):
    first = INFO + j * HALF
    for k in range(NCOL):
        anom[:, k * 128 : (k + 1) * 128] = at[k, first : first + HALF, :]
    sums = lax.dot_general(anom[...], onehot[:DAYS, :], (((1,), (1,)), ((), ())), preferred_element_type=F32)
    return jnp.concatenate(split(sums * inv_row), axis=1)


def row_part(both, n, onehot, taper, anom):
    season = dot(both, onehot[:, n * 512 : (n + 1) * 512])
    for k in range(4 * n, 4 * n + 4):
        steps = slice(k * 128, (k + 1) * 128)
        here = anom[:, steps].astype(F32) - season[:, (k - 4 * n) * 128 : (k - 4 * n + 1) * 128]
        anom[:, steps] = (here * taper[k : k + 1, :]).astype(BF16)


def gather_kernel(
    series, days, lags, at, bp, lagv, onehot, onehot_t, invs, anom, pad,
    held, held_days, held_lags, stage, land, sl, sa, ra, sb, rb, sra, rra, srb, rrb, ssib, rsib,
):
    r = lax.axis_index("row")
    c = lax.axis_index("col")
    loads = [
        pltpu.make_async_copy(series, held, sl.at[0]),
        pltpu.make_async_copy(days, held_days, sl.at[1]),
        pltpu.make_async_copy(lags, held_lags, sl.at[2]),
    ]
    for load in loads:
        load.start()
    barrier = pltpu.get_barrier_semaphore()
    for j in range(1, NROW):
        pl.semaphore_signal(barrier, inc=1, device_id=(lax.rem(r + j, NROW), c), device_id_type=MESH)
    for j in range(1, NCOL):
        pl.semaphore_signal(barrier, inc=1, device_id=(r, lax.rem(c + j, NCOL)), device_id_type=MESH)

    for load in loads:
        load.wait()
    step = lax.broadcasted_iota(jnp.int32, (STEPS, 128), 0)
    lane = lax.broadcasted_iota(jnp.int32, (STEPS, 128), 1)
    day = jnp.zeros((STEPS, 128), jnp.int32)
    for i in range(STEPS):
        day = jnp.where(step == i, held_days[i], day)
    high = jnp.right_shift(day, 8)
    info = jnp.where(lane == 0, high, jnp.where(lane == 1, day - high * 256, 0))
    info = info.astype(F32).astype(BF16)
    for d in range(NROW):
        stage[d, :, :ROWW] = held[:, d * ROWW : (d + 1) * ROWW]
        stage[d, :, ROWW:] = info

    for k in range(NLAG):
        lagv[k : k + 1, :] = jnp.full((1, 128), held_lags[k], jnp.int32).astype(F32)
    pl.semaphore_wait(barrier, NROW + NCOL - 2)

    rows, cols = [], []
    for j in range(1, NROW):
        to = lax.rem(r + j, NROW)
        copy = pltpu.make_async_remote_copy(
            src_ref=stage.at[to],
            dst_ref=land.at[r],
            send_sem=sa.at[j],
            recv_sem=ra.at[j],
            device_id=(to, c),
            device_id_type=MESH,
        )
        copy.start()
        rows.append(copy)
    for j in range(1, NCOL):
        to = lax.rem(c + j, NCOL)
        copy = pltpu.make_async_remote_copy(
            src_ref=held.at[:, pl.ds(pl.multiple_of(to * COLW, 128), COLW)],
            dst_ref=bp.at[c, r],
            send_sem=sb.at[j],
            recv_sem=rb.at[j],
            device_id=(r, to),
            device_id_type=MESH,
        )
        copy.start()
        cols.append(copy)
    land[r] = stage[r]
    bp[c, r] = held[:, pl.ds(pl.multiple_of(c * COLW, 128), COLW)]

    core = lax.rem(c, 2)
    ring_a = Ring(
        lambda s, j: at.at[s, ROWS[j] : ROWS[j + 1]],
        lambda s, j, h: at.at[s, (ROWS[j], MIDS[j])[h] : (MIDS[j], ROWS[j + 1])[h]],
        lambda p, q: p * 8 + q * 2 + core,
        lambda p, q: (r, p * 8 + q * 2 + core),
        c // 8,
        lax.rem(c // 2, 4),
        sra,
        rra,
    )
    ring_b = Ring(
        lambda s, j: bp.at[:, s, :, COLS[j] : COLS[j + 1]],
        lambda s, j, h: bp.at[8 * h : 8 * h + 8, s, :, COLS[j] : COLS[j + 1]],
        lambda p, q: p * 4 + q,
        lambda p, q: (p * 4 + q, c),
        r // 4,
        lax.rem(r, 4),
        srb,
        rrb,
    )
    pa, qa = ring_a.p, ring_a.q
    siblings = {}

    def sibling(j, p, q):
        n = sum(key[0] == j for key in siblings)
        ref = ring_a.view(ring_a.slot(p, q), j)
        copy = pltpu.make_async_remote_copy(
            src_ref=ref,
            dst_ref=ref,
            send_sem=ssib.at[j, n],
            recv_sem=rsib.at[j, n],
            device_id=(r, c + 1 - 2 * core),
            device_id_type=MESH,
        )
        copy.start()
        siblings[j, n] = copy

    def other(j):
        ring_a.other(j)
        ring_b.other(j)

    def near(j):
        for n in (1, 2):
            ring_a.forward(j, n)
            ring_b.forward(j, n)

    def far(j):
        for n in (3, 4):
            ring_a.forward(j, n)
            ring_b.forward(j, n)

    def last(j):
        for n, p in ((5, pa), (7, 1 - pa)):
            ring_a.copies[j, n].wait_recv()
            ring_a.copies[j, n + 1].wait_recv()
            sibling(j, p, ring_a.at(2))
        for n in (5, 6, 7, 8):
            ring_b.copies[j, n].wait_recv()

    for copy in rows:
        copy.wait_recv()
    block = land[...].reshape(NROW * STEPS, ROWW + 128).astype(F32).T
    at[c, :INFO] = block[ROWW:EXT].astype(BF16)
    at[c, INFO:] = block[:ROWW].astype(BF16)
    ring_a.own(0)
    for copy in cols:
        copy.wait_recv()
    ring_b.own(0)
    sibling(0, pa, qa)
    taper = taper_of()
    taper_t = taper.T
    other(0)
    near(0)
    ring_a.own(1)
    ring_b.own(1)
    sibling(0, 1 - pa, qa)
    sibling(0, pa, ring_a.at(-1))
    sibling(0, pa, ring_a.at(1))
    far(0)
    sibling(0, 1 - pa, ring_a.at(-1))
    sibling(0, 1 - pa, ring_a.at(1))
    sibling(1, pa, qa)
    other(1)
    last(0)
    near(1)
    sibling(1, 1 - pa, qa)
    sibling(1, pa, ring_a.at(-1))
    sibling(1, pa, ring_a.at(1))
    for n in range(8):
        siblings[0, n].wait_recv()

    info = at[:, :INFO, :].astype(F32)
    day = info[:, 0, :] * 256.0 + info[:, 1, :]
    day_t = day.T
    down = lax.broadcasted_iota(jnp.int32, (DAYS, 128), 0).astype(F32)
    along = lax.broadcasted_iota(jnp.int32, (128, DAYS), 1).astype(F32)
    count = jnp.zeros((DAYS, 128), F32)
    for k in range(NCOL):
        steps = slice(k * 128, (k + 1) * 128)
        here = jnp.where(down == day[k : k + 1, :], 1.0, 0.0)
        count = count + here
        hot = here.astype(BF16)
        onehot[:DAYS, steps] = hot
        onehot[DAYS:, steps] = hot
        hot = jnp.where(along == day_t[:, k : k + 1], 1.0, 0.0).astype(BF16)
        onehot_t[steps, :DAYS] = hot
        onehot_t[steps, DAYS:] = hot
    inv = 1.0 / jnp.maximum(jnp.sum(count, axis=1, keepdims=True), 1.0)
    invs[...] = jnp.broadcast_to(inv, (DAYS, 128))
    inv_row = invs[...].T[0:1, :]
    far(1)
    sibling(1, 1 - pa, ring_a.at(-1))
    sibling(1, 1 - pa, ring_a.at(1))
    column_part(bp, 0, onehot, onehot_t, inv, taper_t, pad)
    both = row_sums(at, 0, onehot, inv_row, anom)
    last(1)
    for n in range(4):
        row_part(both, n, onehot, taper, anom)
    for n in range(8):
        siblings[1, n].wait_recv()
    for copy in rows + cols + list(siblings.values()) + list(ring_a.copies.values()) + list(ring_b.copies.values()):
        copy.wait_send()


def hbm(x):
    return pltpu.with_memory_space_constraint(x, pltpu.HBM)


HBM = pl.BlockSpec(memory_space=pltpu.HBM)
VMEM = pl.BlockSpec(memory_space=pltpu.VMEM)
DMA = pltpu.SemaphoreType.DMA


def gather(series, day_index, lags):
    return pl.pallas_call(
        gather_kernel,
        out_shape=(
            jax.ShapeDtypeStruct((NCOL, EXT, 128), BF16),
            jax.ShapeDtypeStruct((NCOL, NROW, STEPS, COLW), BF16),
            jax.ShapeDtypeStruct((NLAG, 128), F32),
            jax.ShapeDtypeStruct((2 * DAYS, TIME), BF16),
            jax.ShapeDtypeStruct((TIME, 2 * DAYS), BF16),
            jax.ShapeDtypeStruct((DAYS, 128), F32),
            jax.ShapeDtypeStruct((HALF, TIME), BF16),
            jax.ShapeDtypeStruct((2, TIME + 2 * PAD, 128), F32),
        ),
        in_specs=[HBM, HBM, HBM],
        out_specs=(VMEM,) * 8,
        scratch_shapes=[
            pltpu.VMEM((STEPS, CHANS), BF16),
            pltpu.SMEM((STEPS,), jnp.int32),
            pltpu.SMEM((NLAG,), jnp.int32),
            pltpu.VMEM((NROW, STEPS, ROWW + 128), BF16),
            pltpu.VMEM((NROW, STEPS, ROWW + 128), BF16),
            DMA((3,)),
            DMA((NROW,)),
            DMA((NROW,)),
            DMA((NCOL,)),
            DMA((NCOL,)),
            DMA((2, 9)),
            DMA((2, 9)),
            DMA((2, 9)),
            DMA((2, 9)),
            DMA((2, 8)),
            DMA((2, 8)),
        ],
        compiler_params=pltpu.CompilerParams(
            collective_id=0, has_side_effects=True, vmem_limit_bytes=12 * 2**20
        ),
        name="gather_series",
    )(hbm(series), hbm(day_index), hbm(lags))


def fill(pads, lag, i, held):
    for k in range(NCOL):
        for b in range(NROW):
            to = (k * NROW + b) * 16
            for w in range(3):
                piece = pads[w // 2][w % 2, pl.ds(PAD + b * 256 + k * 16 + lag, 16), :]
                held[to : to + 16, i * COLW + w * 128 : i * COLW + (w + 1) * 128] = piece.astype(BF16)


def cov_kernel(at, bp, lagv, onehot, onehot_t, invs, anom0, pad0, out, anom1, pad1, early, late, done, sems):
    lag = [jnp.max(lagv[k : k + 1, :]).astype(jnp.int32) for k in range(NLAG)]
    taper = taper_of()
    column_part(bp, 1, onehot, onehot_t, invs[:, 0:1], taper.T, pad1)
    both = row_sums(at, 1, onehot, invs[...].T[0:1, :], anom1)
    pads = (pad0, pad1)
    for n in range(4):
        fill(pads, lag[n], n, early)
        row_part(both, n, onehot, taper, anom1)

    copies = []
    for n in range(4):
        group, m = divmod(n, 2)
        slot = n % SLOTS
        if n >= SLOTS:
            copies[n - SLOTS].wait()
        if group == 0:
            for k in range(2 * m, 2 * m + 2):
                fill(pads, lag[GROUP + k], k, late)
        total = dot((anom0, anom1)[m][...], (early, late)[group][...]) * (1.0 / TIME)
        for i in range(GROUP):
            done[slot, i] = total[:, i * COLW : (i + 1) * COLW]
        copy = pltpu.make_async_copy(
            done.at[slot],
            out.at[group * GROUP : (group + 1) * GROUP, m * HALF : (m + 1) * HALF],
            sems.at[slot],
        )
        copy.start()
        copies.append(copy)
    for copy in copies[-SLOTS:]:
        copy.wait()


def covariance(*gathered):
    return pl.pallas_call(
        cov_kernel,
        out_shape=jax.ShapeDtypeStruct((NLAG, ROWW, COLW), F32),
        in_specs=[VMEM] * 8,
        out_specs=HBM,
        scratch_shapes=[
            pltpu.VMEM((HALF, TIME), BF16),
            pltpu.VMEM((1, TIME + 2 * PAD, 128), F32),
            pltpu.VMEM((TIME, GROUP * COLW), BF16),
            pltpu.VMEM((TIME, GROUP * COLW), BF16),
            pltpu.VMEM((SLOTS, GROUP, HALF, COLW), F32),
            DMA((SLOTS,)),
        ],
        compiler_params=pltpu.CompilerParams(vmem_limit_bytes=30 * 2**20),
        name="lagged_covariance",
    )(*gathered)


def shards(series, day_index, lags):
    return covariance(*gather(series, day_index, lags))


def solution(mesh):
    placed = (P(("row", "col"), None), P(("row", "col")), P())
    return jax.shard_map(
        shards, mesh=mesh, in_specs=placed, out_specs=P(None, "row", "col"), check_vma=False
    )
```

time: 54.8 us -> 57 us (1.040)
  Pallas kernels: 54.3 us -> 56.7 us
    pallas_call x1, Pallas kernels: 34.9 us -> 39.3 us  [gather(): pl.pallas_call(gather_kernel, out_shape=(jax.ShapeDtypeStruct((NCOL, EXT,...]
    pallas_call x1, Pallas kernels: 19.4 us -> 17.5 us  [covariance(): pl.pallas_call(cov_kernel, out_shape=jax.ShapeDtypeStruct((NLAG, ROWW, CO...]
where the time goes in v6:
time: 57 us; the launch traced here: 56.9 us
  Pallas kernels  56.7 us (99%)
    pallas_call x1, Pallas kernels, gather(): pl.pallas_call(gather_kernel, out_shape=(jax.ShapeDtypeStruct((NCOL, EXT,...  39.3 us
    pallas_call x1, Pallas kernels, covariance(): pl.pallas_call(cov_kernel, out_shape=jax.ShapeDtypeStruct((NLAG, ROWW, CO...  17.5 us

profile of v6, /device:TPU:1, one launch (start us, length us, event | category | flops | bytes accessed | tf_op | source)
XLA Modules:
  0.0 56.9 jit_solution(16013587943711534525)
XLA Ops:
  0.0 39.3 %gather_series.1 = (bf16[16,784,128]{2,1,0:T(8,128)(2,1)S(1)}, bf16[16,8,16,384]{3,2,1,0:T(8,128)(2,1)S(1)}, f32[8,128]{1,0:T(8,128)S(1)}, bf16[768,2048]{1,0:T(...) custom-call(bf16[16,6144]{1,0:T(8,128)(2,1)} %series.1, ...), custom_call_target="tpu_custom_call" | custom-call | tf_op jit(solution)/shard_map/gather_series/pallas_call | solution.py:324
  39.3 17.5 %lagged_covariance.1 = f32[8,768,384]{2,1,0:T(8,128)} custom-call(bf16[16,784,128]{2,1,0:T(8,128)(2,1)S(1)} %get-tuple-element.13.at, bf16[16,8,16,384]{3,2,1,0:T(8,128)(2,1)S(1)} %get-tuple-element.14.bp, f32[8,128]{1,0:T(8,128)S(1)} %get-tuple-element.15.lagv, bf16[768,2048]{1,0:T(8,128)(2,1)S(1)} %get-tuple-element.16.onehot, ...), custom_call_target="tpu_custom_call" | custom-call | tf_op jit(solution)/shard_map/lagged_covariance/pallas_call | solution.py:406

commit v7 on v5

--- a/solution.py
+++ b/solution.py
@@ -21,7 +21,7 @@
 GROUP = 4
 NPART = 2
 PART = ROWW // NPART
-SLOTS = 3
+SLOTS = 2
 MESH = pl.DeviceIdType.MESH
 F32 = jnp.float32
 BF16 = jnp.bfloat16
@@ -50,9 +50,9 @@
 
     def own(self):
         ref = self.view(self.slot(self.p, self.q))
+        self.copy(0, ref, self.device(1 - self.p, self.q))
         self.copy(1, ref, self.device(self.p, self.at(1)))
         self.copy(2, ref, self.device(self.p, self.at(-1)))
-        self.copy(0, ref, self.device(1 - self.p, self.q))
 
     def other(self):
         self.copies[0].wait_recv()
@@ -72,8 +72,8 @@
 
 
 def gather_kernel(
-    series, days, lags, at, bp, lagv,
-    held, held_days, held_lags, stage, land, sl, sa, ra, sb, rb, sra, rra, srb, rrb, ssib, rsib,
+    series, days, lags, at, bp, lagv, onehot, onehot_t, invs, taper, taper_t,
+    count, held, held_days, held_lags, stage, land, sl, sa, ra, sb, rb, sra, rra, srb, rrb, ssib, rsib,
 ):
     r = lax.axis_index("row")
     c = lax.axis_index("col")
@@ -173,6 +173,27 @@
         copy.start()
         siblings.append(copy)
 
+    down = lax.broadcasted_iota(jnp.int32, (DAYS, 128), 0).astype(F32)
+    along = lax.broadcasted_iota(jnp.int32, (128, DAYS), 1).astype(F32)
+
+    def hot(slot):
+        info = at[slot, ROWW:, :].astype(F32)
+        day = info[0:1] * 256.0 + info[1:2]
+        steps = pl.ds(pl.multiple_of(slot * 128, 128), 128)
+        here = jnp.where(down == day, 1.0, 0.0)
+        count[...] += here
+        here = here.astype(BF16)
+        onehot[:DAYS, steps] = here
+        onehot[DAYS:, steps] = here
+        day_t = jnp.broadcast_to(day, (128, 128)).T[:, 0:1]
+        here = jnp.where(along == day_t, 1.0, 0.0).astype(BF16)
+        onehot_t[steps, :DAYS] = here
+        onehot_t[steps, DAYS:] = here
+
+    def hot_sibling(n, p, q):
+        siblings[n].wait_recv()
+        hot(p * 8 + q * 2 + 1 - core)
+
     for copy in rows:
         copy.wait_recv()
     block = land[...].reshape(NROW * STEPS, ROWW + 128).astype(F32)
@@ -182,31 +203,55 @@
         copy.wait_recv()
     ring_b.own()
     pa, qa = ring_a.p, ring_a.q
+    po = 1 - pa
+    down_q, up_q, far_q = ring_a.at(-1), ring_a.at(1), ring_a.at(2)
     sibling(pa, qa)
+    place = lax.broadcasted_iota(jnp.int32, (NCOL, 128), 1)
+    when = place // STEPS * (NCOL * STEPS) + lax.broadcasted_iota(jnp.int32, (NCOL, 128), 0) * STEPS + place % STEPS
+    wave = 0.5 - 0.5 * jnp.cos(2.0 * math.pi * (when.astype(F32) + 0.5) / TIME)
+    taper[...] = wave
+    taper_t[...] = wave.T
+    count[...] = jnp.zeros((DAYS, 128), F32)
+    hot(c)
     ring_a.other()
     ring_b.other()
-    ring_a.forward(1)
-    ring_a.forward(2)
-    ring_b.forward(1)
-    ring_b.forward(2)
-    sibling(1 - pa, qa)
-    sibling(pa, ring_a.at(-1))
-    sibling(pa, ring_a.at(1))
-    ring_a.forward(3)
-    ring_a.forward(4)
-    ring_b.forward(3)
-    ring_b.forward(4)
-    sibling(1 - pa, ring_a.at(-1))
-    sibling(1 - pa, ring_a.at(1))
-    for pair, first in ((pa, 5), (1 - pa, 7)):
-        ring_a.copies[first].wait_recv()
-        ring_a.copies[first + 1].wait_recv()
-        sibling(pair, ring_a.at(2))
+    for n in (1, 2):
+        ring_a.forward(n)
+        ring_b.forward(n)
+    sibling(po, qa)
+    sibling(pa, down_q)
+    sibling(pa, up_q)
+    hot(ring_a.slot(po, qa))
+    hot(ring_a.slot(pa, down_q))
+    hot(ring_a.slot(pa, up_q))
+    hot_sibling(0, pa, qa)
+    for n in (3, 4):
+        ring_a.forward(n)
+        ring_b.forward(n)
+    sibling(po, down_q)
+    sibling(po, up_q)
+    hot(ring_a.slot(po, down_q))
+    hot(ring_a.slot(po, up_q))
+    for n in (5, 6):
+        ring_a.copies[n].wait_recv()
+    sibling(pa, far_q)
+    hot(ring_a.slot(pa, far_q))
+    hot_sibling(1, po, qa)
+    hot_sibling(2, pa, down_q)
+    hot_sibling(3, pa, up_q)
+    for n in (7, 8):
+        ring_a.copies[n].wait_recv()
+    sibling(po, far_q)
+    hot(ring_a.slot(po, far_q))
+    hot_sibling(4, po, down_q)
+    hot_sibling(5, po, up_q)
+    hot_sibling(6, pa, far_q)
+    hot_sibling(7, po, far_q)
+    inv = 1.0 / jnp.maximum(jnp.sum(count[...], axis=1, keepdims=True), 1.0)
+    invs[...] = jnp.broadcast_to(inv, (DAYS, 128))
     for n in (5, 6, 7, 8):
         ring_b.copies[n].wait_recv()
-    for copy in siblings:
-        copy.wait()
-    for copy in rows + cols + list(ring_a.copies.values()) + list(ring_b.copies.values()):
+    for copy in rows + cols + siblings + list(ring_a.copies.values()) + list(ring_b.copies.values()):
         copy.wait_send()
 
 
@@ -226,10 +271,16 @@
             jax.ShapeDtypeStruct((NCOL, EXT, 128), BF16),
             jax.ShapeDtypeStruct((NCOL, NROW, STEPS, COLW), BF16),
             jax.ShapeDtypeStruct((NLAG, 128), F32),
+            jax.ShapeDtypeStruct((2 * DAYS, TIME), BF16),
+            jax.ShapeDtypeStruct((TIME, 2 * DAYS), BF16),
+            jax.ShapeDtypeStruct((DAYS, 128), F32),
+            jax.ShapeDtypeStruct((NCOL, 128), F32),
+            jax.ShapeDtypeStruct((128, NCOL), F32),
         ),
         in_specs=[HBM, HBM, HBM],
-        out_specs=(VMEM, VMEM, VMEM),
+        out_specs=(VMEM,) * 8,
         scratch_shapes=[
+            pltpu.VMEM((DAYS, 128), F32),
             pltpu.VMEM((STEPS, CHANS), BF16),
             pltpu.SMEM((STEPS,), jnp.int32),
             pltpu.SMEM((NLAG,), jnp.int32),
@@ -272,32 +323,12 @@
     return high, (x - high.astype(F32)).astype(BF16)
 
 
-def cov_kernel(lagv, at, bp, out, anom, onehot, onehot_t, pad, early, late, done, sems):
+def cov_kernel(at, bp, lagv, onehot, onehot_t, invs, taper, taper_t, out, anom, pad, early, late, done, sems):
     lag = [jnp.max(lagv[k : k + 1, :]).astype(jnp.int32) for k in range(NLAG)]
-    place = lax.broadcasted_iota(jnp.int32, (NCOL, 128), 1)
-    when = place // STEPS * (NCOL * STEPS) + lax.broadcasted_iota(jnp.int32, (NCOL, 128), 0) * STEPS + place % STEPS
-    taper = 0.5 - 0.5 * jnp.cos(2.0 * math.pi * (when.astype(F32) + 0.5) / TIME)
-    taper_t = taper.T
-
-    info = at[:, ROWW:, :].astype(F32)
-    day = info[:, 0, :] * 256.0 + info[:, 1, :]
-    day_t = day.T
-    down = lax.broadcasted_iota(jnp.int32, (DAYS, 128), 0).astype(F32)
-    along = lax.broadcasted_iota(jnp.int32, (128, DAYS), 1).astype(F32)
-    count = jnp.zeros((DAYS, 128), F32)
+    inv_col = invs[:, 0:1]
+    inv_row = invs[...].T[0:1, :]
     for k in range(NCOL):
-        steps = slice(k * 128, (k + 1) * 128)
-        anom[:, steps] = at[k, :ROWW, :]
-        here = jnp.where(down == day[k : k + 1, :], 1.0, 0.0)
-        count = count + here
-        hot = here.astype(BF16)
-        onehot[:DAYS, steps] = hot
-        onehot[DAYS:, steps] = hot
-        hot = jnp.where(along == day_t[:, k : k + 1], 1.0, 0.0).astype(BF16)
-        onehot_t[steps, :DAYS] = hot
-        onehot_t[steps, DAYS:] = hot
-    inv_col = 1.0 / jnp.maximum(jnp.sum(count, axis=1, keepdims=True), 1.0)
-    inv_row = jnp.broadcast_to(inv_col, (DAYS, 128)).T[0:1, :]
+        anom[:, k * 128 : (k + 1) * 128] = at[k, :ROWW, :]
 
     sums = dot(onehot[:DAYS, :], bp[...].reshape(TIME, COLW))
     both = jnp.concatenate(split(sums * inv_col), axis=0)
@@ -343,25 +374,23 @@
         copy.wait()
 
 
-def covariance(at, bp, lagv):
+def covariance(*gathered):
     return pl.pallas_call(
         cov_kernel,
         out_shape=jax.ShapeDtypeStruct((NLAG, ROWW, COLW), F32),
-        in_specs=[VMEM] * 3,
+        in_specs=[VMEM] * 8,
         out_specs=HBM,
         scratch_shapes=[
             pltpu.VMEM((ROWW, TIME), BF16),
-            pltpu.VMEM((2 * DAYS, TIME), BF16),
-            pltpu.VMEM((TIME, 2 * DAYS), BF16),
             pltpu.VMEM((3, TIME + 2 * PAD, 128), F32),
             pltpu.VMEM((TIME, GROUP * COLW), BF16),
             pltpu.VMEM((TIME, GROUP * COLW), BF16),
             pltpu.VMEM((SLOTS, GROUP, PART, COLW), F32),
             DMA((SLOTS,)),
         ],
-        compiler_params=pltpu.CompilerParams(vmem_limit_bytes=48 * 2**20),
+        compiler_params=pltpu.CompilerParams(vmem_limit_bytes=36 * 2**20),
         name="lagged_covariance",
-    )(lagv, at, bp)
+    )(*gathered)
 
 
 def shards(series, day_index, lags):

time: 54.8 us -> 58 us (1.058)
  Pallas kernels: 54.3 us -> 57.7 us
    pallas_call x1, Pallas kernels: 34.9 us -> 37.8 us  [gather(): pl.pallas_call(gather_kernel, out_shape=(jax.ShapeDtypeStruct((NCOL, EXT,...]
where the time goes in v7:
time: 58 us; the launch traced here: 57.8 us
  Pallas kernels  57.7 us (99%)
    pallas_call x1, Pallas kernels, gather(): pl.pallas_call(gather_kernel, out_shape=(jax.ShapeDtypeStruct((NCOL, EXT,...  37.8 us
    pallas_call x1, Pallas kernels, covariance(): pl.pallas_call(cov_kernel, out_shape=jax.ShapeDtypeStruct((NLAG, ROWW, CO...  19.9 us

profile of v7, /device:TPU:1, one launch (start us, length us, event | category | flops | bytes accessed | tf_op | source)
XLA Modules:
  0.0 57.8 jit_solution(8769584348924388745)
XLA Ops:
  0.0 37.8 %gather_series.1 = (bf16[16,784,128]{2,1,0:T(8,128)(2,1)S(1)}, bf16[16,8,16,384]{3,2,1,0:T(8,128)(2,1)S(1)}, f32[8,128]{1,0:T(8,128)S(1)}, bf16[768,2048]{1,0:T(...) custom-call(bf16[16,6144]{1,0:T(8,128)(2,1)} %series.1, ...), custom_call_target="tpu_custom_call" | custom-call | tf_op jit(solution)/shard_map/gather_series/pallas_call | solution.py:268
  37.8 19.9 %lagged_covariance.1 = f32[8,768,384]{2,1,0:T(8,128)} custom-call(bf16[16,784,128]{2,1,0:T(8,128)(2,1)S(1)} %get-tuple-element.13.at, bf16[16,8,16,384]{3,2,1,0:T(8,128)(2,1)S(1)} %get-tuple-element.14.bp, f32[8,128]{1,0:T(8,128)S(1)} %get-tuple-element.15.lagv, bf16[768,2048]{1,0:T(8,128)(2,1)S(1)} %get-tuple-element.16.onehot, ...), custom_call_target="tpu_custom_call" | custom-call | tf_op jit(solution)/shard_map/lagged_covariance/pallas_call | solution.py:378

commit v8 on v5

--- a/solution.py
+++ b/solution.py
@@ -255,12 +255,12 @@
 
 
 def fill(pad, lag, i, held):
-    for k in range(NCOL):
-        for b in range(NROW):
-            to = (k * NROW + b) * 16
-            for w in range(3):
-                piece = pad[w, pl.ds(PAD + b * 256 + k * 16 + lag, 16), :]
-                held[to : to + 16, i * COLW + w * 128 : i * COLW + (w + 1) * 128] = piece.astype(BF16)
+    for b in range(NROW):
+        for w in range(3):
+            piece = pad[w, pl.ds(PAD + b * 256 + lag, 256), :].astype(BF16)
+            for k in range(NCOL):
+                to = (k * NROW + b) * 16
+                held[to : to + 16, i * COLW + w * 128 : i * COLW + (w + 1) * 128] = piece[k * 16 : (k + 1) * 16]
 
 
 def dot(a, b):
@@ -313,10 +313,13 @@
                 for w in range(3):
                     pad[w, row : row + 16, :] = here[b * 16 : (b + 1) * 16, w * 128 : (w + 1) * 128]
 
+    fill(pad, lag[0], 0, early)
+    fill(pad, lag[1], 1, early)
     sums = lax.dot_general(anom[...], onehot[:DAYS, :], (((1,), (1,)), ((), ())), preferred_element_type=F32)
     both = jnp.concatenate(split(sums * inv_row), axis=1)
     for n in range(4):
-        fill(pad, lag[n], n, early)
+        if n < 2:
+            fill(pad, lag[n + 2], n + 2, early)
         season = dot(both, onehot[:, n * 512 : (n + 1) * 512])
         for k in range(4 * n, 4 * n + 4):
             steps = slice(k * 128, (k + 1) * 128)

time: 54.8 us -> 54.9 us (level)
  no operation moved by 1% of the time
where the time goes in v8:
time: 54.9 us; the launch traced here: 54.6 us
  Pallas kernels  54.4 us (99%)
    pallas_call x1, Pallas kernels, gather(): pl.pallas_call(gather_kernel, out_shape=(jax.ShapeDtypeStruct((NCOL, EXT,...  34.9 us
    pallas_call x1, Pallas kernels, covariance(): pl.pallas_call(cov_kernel, out_shape=jax.ShapeDtypeStruct((NLAG, ROWW, CO...  19.5 us

profile of v8, /device:TPU:1, one launch (start us, length us, event | category | flops | bytes accessed | tf_op | source)
XLA Modules:
  0.0 54.6 jit_solution(7287765249367298045)
XLA Ops:
  0.0 34.9 %gather_series.1 = (bf16[16,784,128]{2,1,0:T(8,128)(2,1)S(1)}, bf16[16,8,16,384]{3,2,1,0:T(8,128)(2,1)S(1)}, f32[8,128]{1,0:T(8,128)S(1)}) custom-call(bf16[16,6144]{1,0:T(8,128)(2,1)} %series.1, s32[16]{0:T(128)} %days.1, s32[8]{0:T(128)} %lags.1), custom_call_target="tpu_custom_call" | custom-call | tf_op jit(solution)/shard_map/gather_series/pallas_call | solution.py:223
  34.9 19.5 %lagged_covariance.1 = f32[8,768,384]{2,1,0:T(8,128)} custom-call(f32[8,128]{1,0:T(8,128)S(1)} %get-tuple-element.8.lagv, bf16[16,784,128]{2,1,0:T(8,128)(2,1)S(1)} %get-tuple-element.9.at, bf16[16,8,16,384]{3,2,1,0:T(8,128)(2,1)S(1)} %get-tuple-element.10.bp), custom_call_target="tpu_custom_call" | custom-call | tf_op jit(solution)/shard_map/lagged_covariance/pallas_call | solution.py:350

commit v9 on v8

--- a/solution.py
+++ b/solution.py
@@ -192,16 +192,17 @@
     sibling(1 - pa, qa)
     sibling(pa, ring_a.at(-1))
     sibling(pa, ring_a.at(1))
-    ring_a.forward(3)
-    ring_a.forward(4)
-    ring_b.forward(3)
-    ring_b.forward(4)
+    for n in (5, 6):
+        ring_a.copies[n].wait_recv()
+    ring_a.copy(7, ring_a.view(ring_a.slot(pa, ring_a.at(2))), ring_a.device(1 - pa, qa))
+    sibling(pa, ring_a.at(2))
+    for n in (3, 4):
+        ring_a.copies[n].wait_recv()
+        ring_b.forward(n)
     sibling(1 - pa, ring_a.at(-1))
     sibling(1 - pa, ring_a.at(1))
-    for pair, first in ((pa, 5), (1 - pa, 7)):
-        ring_a.copies[first].wait_recv()
-        ring_a.copies[first + 1].wait_recv()
-        sibling(pair, ring_a.at(2))
+    ring_a.copies[7].wait_recv()
+    sibling(1 - pa, ring_a.at(2))
     for n in (5, 6, 7, 8):
         ring_b.copies[n].wait_recv()
     for copy in siblings:

time: 54.9 us -> 55 us (level)
  no operation moved by 1% of the time
where the time goes in v9:
time: 55 us; the launch traced here: 54.9 us
  Pallas kernels  54.7 us (99%)
    pallas_call x1, Pallas kernels, gather(): pl.pallas_call(gather_kernel, out_shape=(jax.ShapeDtypeStruct((NCOL, EXT,...  35.3 us
    pallas_call x1, Pallas kernels, covariance(): pl.pallas_call(cov_kernel, out_shape=jax.ShapeDtypeStruct((NLAG, ROWW, CO...  19.5 us

profile of v9, /device:TPU:1, one launch (start us, length us, event | category | flops | bytes accessed | tf_op | source)
XLA Modules:
  0.0 54.9 jit_solution(6247357309198114746)
XLA Ops:
  0.0 35.3 %gather_series.1 = (bf16[16,784,128]{2,1,0:T(8,128)(2,1)S(1)}, bf16[16,8,16,384]{3,2,1,0:T(8,128)(2,1)S(1)}, f32[8,128]{1,0:T(8,128)S(1)}) custom-call(bf16[16,6144]{1,0:T(8,128)(2,1)} %series.1, s32[16]{0:T(128)} %days.1, s32[8]{0:T(128)} %lags.1), custom_call_target="tpu_custom_call" | custom-call | tf_op jit(solution)/shard_map/gather_series/pallas_call | solution.py:224
  35.3 19.5 %lagged_covariance.1 = f32[8,768,384]{2,1,0:T(8,128)} custom-call(f32[8,128]{1,0:T(8,128)S(1)} %get-tuple-element.8.lagv, bf16[16,784,128]{2,1,0:T(8,128)(2,1)S(1)} %get-tuple-element.9.at, bf16[16,8,16,384]{3,2,1,0:T(8,128)(2,1)S(1)} %get-tuple-element.10.bp), custom_call_target="tpu_custom_call" | custom-call | tf_op jit(solution)/shard_map/lagged_covariance/pallas_call | solution.py:351
